TPU v7x, 128 devices: a whole 4x4x4 slice. The times are simulated.
128 devices in a mesh: team: 4 (over z_lo, core), row: 32 (over x, z_hi, y).
Axes of the slice: x: 4, y: 4, z: 4 (z_hi: 2, z_lo: 2; z = z_hi * 2 + z_lo), core: 2. Of those that a mesh axis runs over, the one named last changes fastest.
Arguments:
- features: bfloat16 [65536, 128], P(('team', 'row')), may hold values from -6 to 6
- tile_values: bfloat16 [512, 12, 256, 256], P(('team', 'row')), may hold values from 0 to 0.09375, as said below
- tile_row: int32 [512, 12], P(('team', 'row')), may hold values from 0 to 1
- tile_col: int32 [512, 12], P(('team', 'row')), may hold values from 0 to 63
- tile_count: int32 [512], P(('team', 'row')), may hold values from 1 to 12, as said below
- weight: bfloat16 [128, 256], replicated, may hold values from -0.5 to 0.5
- bias: float32 [256], replicated, may hold values from -1.5 to 1.5
- cotangent: bfloat16 [65536, 256], P(('team', 'row')), may hold values from -0.0234375 to 0.0234375
Outputs:
- hidden: bfloat16 [65536, 256], P(('team', 'row'))
- weight_grad: float32 [128, 256], replicated
- bias_grad: float32 [256], replicated
Inputs may be any that keep to these rules, and one draw needn't show every extreme that they name: Live tiles stand in the first tile_count[g] slots of group g. In every draw some owner has 12 live tiles in each of its 4 groups. `tile_values`: every entry is a whole multiple of 1 / 32; most entries are zero.
All inputs are finite; a program needn't handle non-finite values.
Results may differ from a plain program's by a relative error of at most 0.0052.
Values may be sent and summed in bfloat16 or wider, within the bound.
No kernel may reach another device: no remote copies, remote signals or barrier semaphores. Data moves between devices by JAX's collectives and lax.ppermute only.
A program may use at most 128 MiB of HBM per device.

v0:
```python
import jax
import jax.numpy as jnp
from jax import lax
from jax.sharding import PartitionSpec as P


def gelu_parts(values):
    gelu_coef = 0.7978845608
    tangent_h = jnp.tanh(gelu_coef * (values + 0.044715 * values * values * values))
    result = 0.5 * values * (1.0 + tangent_h)
    derive = 0.5 * (1.0 + tangent_h) + 0.5 * values * (1.0 - tangent_h * tangent_h) * gelu_coef * (
        1.0 + 3.0 * 0.044715 * values * values
    )
    return (result, derive)


def local(features, tile_values, tile_row, tile_col, tile_count, weight, bias, cotangent):
    team_count = lax.axis_size("team")
    block_size = tile_values.shape[2]
    slot_count = tile_values.shape[1]
    rows_dev = features.shape[0]
    in_width = features.shape[1]
    row_blocks = rows_dev // block_size
    slot_ids = jnp.arange(slot_count, dtype=jnp.int32)
    block_ids = jnp.arange(row_blocks, dtype=jnp.int32)
    total = jnp.zeros((row_blocks, block_size, in_width), jnp.float32)
    gathered = lax.all_gather(features, ("team", "row"), axis=0, tiled=True)
    panel_rows = gathered.shape[0] // team_count
    for panel_id in range(team_count):
        feature_panel = gathered[panel_id * panel_rows : (panel_id + 1) * panel_rows]
        panel_blocks = feature_panel.reshape(-1, block_size, in_width)
        tiles = lax.dynamic_index_in_dim(tile_values, panel_id, 0, False)
        row_index = lax.dynamic_index_in_dim(tile_row, panel_id, 0, False)
        col_index = lax.dynamic_index_in_dim(tile_col, panel_id, 0, False)
        count = lax.dynamic_index_in_dim(tile_count, panel_id, 0, False)
        picked = jnp.take(panel_blocks, col_index, axis=0)
        products = jnp.einsum("sij,sjf->sif", tiles, picked, preferred_element_type=jnp.float32)
        live_mask = slot_ids < count
        row_select = ((row_index[None, :] == block_ids[:, None]) & live_mask[None, :]).astype(
            jnp.float32
        )
        total = total + jnp.einsum(
            "rs,sif->rif", row_select, products, precision=lax.Precision.HIGHEST
        )
    aggregated = total.reshape(rows_dev, in_width).astype(jnp.bfloat16)
    pre = jnp.dot(aggregated, weight, preferred_element_type=jnp.float32) + bias
    result, derive = gelu_parts(pre)
    hidden = result.astype(jnp.bfloat16)
    slope = cotangent.astype(jnp.float32) * derive
    slope_half = slope.astype(jnp.bfloat16)
    weight_part = lax.dot_general(
        aggregated, slope_half, (((0,), (0,)), ((), ())), preferred_element_type=jnp.float32
    )
    bias_part = jnp.sum(slope, axis=0)
    summed = lax.psum((weight_part, bias_part), ("team", "row"))
    return (hidden, summed[0], summed[1])


def solution(mesh):
    in_specs = (
        P(("team", "row"), None),
        P(("team", "row"), None, None, None),
        P(("team", "row"), None),
        P(("team", "row"), None),
        P(("team", "row")),
        P(),
        P(),
        P(("team", "row"), None),
    )
    out_specs = (P(("team", "row"), None), P(), P())
    return jax.shard_map(local, mesh=mesh, in_specs=in_specs, out_specs=out_specs, check_vma=False)
```

profile of v0, /device:TPU:1, one launch (start us, length us, event | category | flops | bytes accessed | tf_op | source)
XLA Modules:
  0.0 543.4 jit_solution(10520821963333200717)
XLA Ops:
  7.2 0.0 copy-start
  7.2 0.0 all-gather.2.cloned.1.call-start
  7.2 0.7 all-gather.2.cloned.1.call-update
  7.9 0.0 all-reduce.2.cloned.1.call-start
  8.0 1.4 fusion.83
  9.4 0.6 iota_compare_fusion
  10.0 0.7 iota_compare_fusion.2
  10.7 0.7 iota_compare_fusion.3
  11.3 0.6 iota_compare_fusion.1
  12.0 0.8 compare_and_fusion
  12.8 0.8 slice_bitcast_fusion
  13.7 326.5 %all-gather.2.cloned.1.call-done = bf16[65536,128]{1,0:T(8,128)(2,1)} async-done(((bf16[512,128]{1,0:T(8,128)(2,1)}), bf16[65536,128]{1,0:T(8,128)(2,1)}) %all-gather.2.cloned.1.call-update) | async-done | bytes 16777232 | tf_op jit(solution)/shard_map/all_gather | solution.py:27
  340.1 12.1 %fusion.82 = (bf16[16384,128]{1,0:T(8,128)(2,1)}, bf16[16384,128]{1,0:T(8,128)(2,1)}, bf16[16384,128]{1,0:T(8,128)(2,1)}, bf16[16384,128]{1,0:T(8,128)(2,1)}) fusion(bf16[65536,128]{1,0:T(8,128)(2,1)} %all-gather.2.cloned.1.call-done), kind=kLoop, calls=%fused_computation.101 | loop fusion | bytes 33554432 | tf_op jit(solution)/shard_map/slice | solution.py:30
  352.3 2.9 gather_fusion.1
  355.2 2.4 fusion.12
  357.6 2.0 copy.13
  359.5 2.9 gather_fusion
  362.4 3.6 fusion.14
  366.0 2.1 copy.12
  368.2 2.9 gather_fusion.3
  371.0 3.6 fusion.8
  374.6 2.9 copy.15
  377.6 2.9 gather_fusion.2
  380.5 3.6 fusion.10
  384.0 2.9 copy.14
  387.0 0.0 copy-start.1
  387.0 2.5 fusion.4
  389.5 0.0 copy-start.2
  389.5 0.9 fusion.20
  390.4 0.0 copy-done.1
  390.4 0.0 copy-start.3
  390.4 0.0 copy-start.4
  390.4 0.9 fusion.23
  391.3 0.0 copy-done.2
  391.3 0.9 fusion.29
  392.2 0.0 copy-done
  392.3 0.0 copy-done.3
  392.3 0.0 copy-done.4
  392.3 1.3 fusion.80
  393.5 0.9 fusion.50
  394.4 0.0 all-reduce.2.cloned.1.call-update
  394.4 65.8 %psum.15 = f32[256]{0:T(256)} all-reduce(f32[256]{0:T(256)S(1)} %get-tuple-element.4), channel_id=1, replica_groups=mesh['team'=4,'row'=32] {'team','row'}, use_global_device_ids=true, to_apply=%region_2.4 | all-reduce | flops 256 | bytes 2048 | tf_op jit(solution)/shard_map/psum | solution.py:55
  460.2 74.8 %all-reduce.2.cloned.1.call-done = f32[128,256]{1,0:T(8,128)} async-done(((f32[128,256]{1,0:T(8,128)}), f32[128,256]{1,0:T(8,128)}) %all-reduce.2.cloned.1.call-update) | async-done | bytes 131088 | tf_op jit(solution)/shard_map/psum | solution.py:55
  535.0 1.6 copy.17
  (3 shorter events, 0.0 us)
Async XLA Ops:
  7.2 385.1 %copy-start = (bf16[128,256]{1,0:T(8,128)(2,1)S(1)}, bf16[128,256]{1,0:T(8,128)(2,1)}, u32[]{:S(2)}) copy-start(bf16[128,256]{1,0:T(8,128)(2,1)} %param.15) | copy-start | bytes 196612
  7.2 333.0 %all-gather.2.cloned.1.call-start = ((), (), s32[]{:S(2)}) async-start(), calls=%async_computation | async-start | bytes 16908288 | tf_op jit(solution)/shard_map/all_gather | solution.py:27
  7.9 527.1 %all-reduce.2.cloned.1.call-start = ((), (), s32[]{:S(2)}) async-start(), calls=%async_computation.1 | async-start | bytes 262144 | tf_op jit(solution)/shard_map/psum | solution.py:55
  387.0 3.4 copy-start.1
  389.5 1.8 copy-start.2
  390.4 1.8 copy-start.3
  390.4 1.8 copy-start.4
Sparse Core Ops, SparseCore 0:
  9.7 330.3 all-gather.1
  394.6 140.3 all-reduce.1
where the time goes:
time: 544 us; the launch traced here: 543 us
  waiting for transfers between devices  402 us (74%)
  blocking collectives  65.8 us (12%)
  local copies, waits for them, and re-layouts  37.5 us (7%)
  matrix products  20.4 us (4%)
  between operations  14.2 us (3%)
    all_gather x1, waiting for transfers between devices, local(): gathered = lax.all_gather(features, ('team', 'row'), axis=0, tiled=True)  326 us
    psum x1, waiting for transfers between devices, local(): summed = lax.psum((weight_part, bias_part), ('team', 'row'))  74.8 us
    psum x1, blocking collectives, local(): summed = lax.psum((weight_part, bias_part), ('team', 'row'))  65.8 us
    dot_general x4, matrix products, local(): jnp.einsum('sij,sjf->sif', tiles, picked, preferred_element_type=jnp.floa...  13.1 us
    slice x1, local copies, waits for them, and re-layouts, local(): feature_panel = gathered[panel_id * panel_rows:(panel_id + 1) * panel_rows]  12.1 us
    gather x4, local copies, waits for them, and re-layouts, local(): picked = jnp.take(panel_blocks, col_index, axis=0)  11.5 us
  transfers between devices with their start and end apart: 2, of which 2 were waited for; matrix products, arithmetic and copies ran while one was open for 1% of the time, Pallas kernels for 0%

commit v1 on v0

v1 whole, which is shorter than its diff:
```python
import functools

import jax
import jax.numpy as jnp
from jax import lax
from jax.experimental import pallas as pl
from jax.experimental.pallas import tpu as pltpu
from jax.sharding import Mesh, PartitionSpec as P

AXES = ("zlo", "core", "x", "zhi", "y")
AXIS_SIZES = (2, 2, 4, 2, 4)
PLANE = ("x", "y")
PEERS = 16


def z_of(index):
    return (index % 2) * 2 + index // 2


def ring(value, axis, step):
    if axis == "z":
        pairs = [(i, z_of((z_of(i) + step) % 4)) for i in range(4)]
        return lax.ppermute(value, ("zlo", "zhi"), pairs)
    size = lax.axis_size(axis)
    return lax.ppermute(value, axis, [(i, (i + step) % size) for i in range(size)])


def gather_kernel(need_ref, own_ref, one_ref, two_ref, three_ref, other_ref, out_ref, table_ref):
    part = own_ref.shape[0]
    for at, piece in enumerate((own_ref, one_ref, two_ref, three_ref)):
        table_ref[at * part : (at + 1) * part] = piece[...]
    table_ref[4 * part :] = other_ref[...]
    slots = out_ref.shape[1]

    def one_peer(peer, carry):
        for slot in range(slots):
            out_ref[peer, slot] = table_ref[need_ref[peer, slot]]
        return carry

    lax.fori_loop(0, out_ref.shape[0], one_peer, 0)


def gather_slices(need, own, one, two, three, other, slots):
    part, height, width = own.shape
    vmem = pl.BlockSpec(memory_space=pltpu.VMEM)
    return pl.pallas_call(
        gather_kernel,
        out_shape=jax.ShapeDtypeStruct((PEERS, slots, height, width), own.dtype),
        grid_spec=pltpu.PrefetchScalarGridSpec(
            num_scalar_prefetch=1,
            grid=(),
            in_specs=[vmem] * 5,
            out_specs=vmem,
            scratch_shapes=[pltpu.VMEM((8 * part, height, width), own.dtype)],
        ),
        compiler_params=pltpu.CompilerParams(vmem_limit_bytes=24 * 1024 * 1024),
        name="pick_slices",
    )(need, own, one, two, three, other)


def gelu_parts(values):
    gelu_coef = 0.7978845608
    tangent_h = jnp.tanh(gelu_coef * (values + 0.044715 * values * values * values))
    result = 0.5 * values * (1.0 + tangent_h)
    derive = 0.5 * (1.0 + tangent_h) + 0.5 * values * (1.0 - tangent_h * tangent_h) * gelu_coef * (
        1.0 + 3.0 * 0.044715 * values * values
    )
    return (result, derive)


def layer_kernel(
    row_ref, count_ref, tiles_ref, slices_ref, weight_ref, bias_ref, cotangent_ref, hidden_ref, grad_ref, total_ref
):
    group = pl.program_id(0)
    slots, block = tiles_ref.shape[1], tiles_ref.shape[2]

    @pl.when(group == 0)
    def _():
        total_ref[...] = jnp.zeros_like(total_ref)

    count = count_ref[group]
    for slot in range(slots):

        @pl.when(slot < count)
        def _():
            picked = jnp.concatenate([slices_ref[i, slot] for i in range(PEERS)], axis=0)
            product = jnp.dot(tiles_ref[0, slot], picked, preferred_element_type=jnp.float32)
            rows = pl.ds(pl.multiple_of(row_ref[group, slot] * block, block), block)
            total_ref[rows, :] += product

    @pl.when(group == pl.num_programs(0) - 1)
    def _():
        aggregated = total_ref[...].astype(jnp.bfloat16)
        pre = jnp.dot(aggregated, weight_ref[...], preferred_element_type=jnp.float32) + bias_ref[...]
        result, derive = gelu_parts(pre)
        hidden_ref[...] = result.astype(jnp.bfloat16)
        slope = cotangent_ref[...].astype(jnp.float32) * derive
        weight_part = lax.dot_general(
            aggregated,
            slope.astype(jnp.bfloat16),
            (((0,), (0,)), ((), ())),
            preferred_element_type=jnp.float32,
        )
        bias_part = jnp.sum(slope, axis=0, keepdims=True)
        grad_ref[:, :16, :] = weight_part.reshape(8, 16, weight_part.shape[1])
        first = lax.broadcasted_iota(jnp.int32, (8, bias_part.shape[1]), 0) == 0
        grad_ref[:, 16:, :] = jnp.zeros((8, 8, bias_part.shape[1]), jnp.float32)
        grad_ref[0, 16:, :] = jnp.where(first, bias_part, 0.0)


def layer(rows, counts, tiles, slices, weight, bias, cotangent):
    groups, slots, block, _ = tiles.shape
    nodes, out_width = cotangent.shape
    height, width = slices.shape[2:]
    whole = lambda shape: pl.BlockSpec(shape, lambda g, *_: (0,) * len(shape))
    return pl.pallas_call(
        layer_kernel,
        out_shape=(
            jax.ShapeDtypeStruct((nodes, out_width), jnp.bfloat16),
            jax.ShapeDtypeStruct((8, 24, out_width), jnp.float32),
        ),
        grid_spec=pltpu.PrefetchScalarGridSpec(
            num_scalar_prefetch=2,
            grid=(groups,),
            in_specs=[
                pl.BlockSpec((1, slots, block, block), lambda g, *_: (g, 0, 0, 0)),
                pl.BlockSpec((PEERS, slots, height, width), lambda g, *_: (0, g, 0, 0)),
                whole(weight.shape),
                whole((1, out_width)),
                whole(cotangent.shape),
            ],
            out_specs=(whole((nodes, out_width)), whole((8, 24, out_width))),
            scratch_shapes=[pltpu.VMEM((nodes, width), jnp.float32)],
        ),
        compiler_params=pltpu.CompilerParams(
            dimension_semantics=("arbitrary",), vmem_limit_bytes=32 * 1024 * 1024
        ),
        name="layer",
    )(rows, counts, tiles, slices, weight, bias.reshape(1, -1), cotangent)


def exchange(value, axis):
    one, two, three = (ring(value, axis, step) for step in (1, 2, 3))
    return (value + two) + (one + three)


def pick(stack, index):
    return lax.dynamic_index_in_dim(stack, index, 0, False)


def sum_over_devices(grad):
    core = lax.axis_index("core")
    depth = lax.axis_index("zhi") * 2 + lax.axis_index("zlo")
    halves = grad.reshape((2, 4) + grad.shape[1:])
    half = pick(halves, core) + ring(pick(halves, 1 - core), "core", 1)
    quarter = pick(half, depth)
    for step in (1, 2, 3):
        quarter = quarter + ring(pick(half, (depth + step) % 4), "z", step)
    quarter = exchange(quarter, "x")
    quarter = exchange(quarter, "y")
    stack = jnp.stack([quarter] + [ring(quarter, "z", step) for step in (1, 2, 3)])
    other = ring(stack, "core", 1)
    first, second = jnp.where(core == 0, stack, other), jnp.where(core == 0, other, stack)
    order = (depth - jnp.arange(4)) % 4
    both = jnp.stack([first, second])
    return jnp.take(both, order, axis=1).reshape(grad.shape)


def local(features, tile_values, tile_row, tile_col, tile_count, weight, bias, cotangent):
    groups, slots, block, _ = tile_values.shape
    width = features.shape[1]
    height = block // PEERS
    needed = groups * slots
    core = lax.axis_index("core")
    depth = lax.axis_index("zhi") * 2 + lax.axis_index("zlo")

    team = lax.broadcasted_iota(jnp.int32, (groups, slots), 0)
    holder, part = tile_col // 2, tile_col % 2
    there = ((holder // 4) % 2) * 2 + team // 2
    place = ((holder // 8) * 4 + holder % 4) * 2 + part
    turn = (team % 2) ^ core
    need = ((turn * 4 + (there - depth) % 4) * (2 * PEERS) + place).astype(jnp.bfloat16).reshape(1, needed)
    need = jnp.broadcast_to(jnp.pad(need, ((0, 0), (0, width - needed))), (height, width))

    mine = features.reshape(-1, PEERS, height, width).transpose(1, 0, 2, 3)
    lists = jnp.broadcast_to(need[None, None], (PEERS, 1, height, width))
    dealt = lax.all_to_all(jnp.concatenate([mine, lists], axis=1), PLANE, 0, 0)
    own = dealt[:, :2].reshape(2 * PEERS, height, width)
    wanted = dealt[:, 2, 0, :needed].astype(jnp.int32)

    one, two, three = (ring(own, "z", -step) for step in (1, 2, 3))
    other = ring(jnp.concatenate([own, one, two, three], axis=0), "core", 1)

    picked = gather_slices(wanted, own, one, two, three, other, needed)
    slices = lax.all_to_all(picked, PLANE, 0, 0)

    hidden, grad = layer(tile_row, tile_count, tile_values, slices, weight, bias, cotangent)
    summed = sum_over_devices(grad)
    weight_grad = summed[:, :16].reshape(weight.shape)
    return (hidden, weight_grad, summed[0, 16])


def solution(mesh):
    fine = Mesh(mesh.devices.reshape(AXIS_SIZES), AXES)
    nodes = P(AXES)
    in_specs = (nodes, nodes, nodes, nodes, nodes, P(), P(), nodes)
    return jax.shard_map(
        local, mesh=fine, in_specs=in_specs, out_specs=(nodes, P(), P()), check_vma=False
    )
```

time: 544 us -> 132 us (0.24)
  waiting for transfers between devices: 402 us -> 59.9 us
  blocking collectives: 65.8 us -> 14.5 us
  starting transfers between devices: 0.08 us -> 40.2 us
  local copies, waits for them, and re-layouts: 37.5 us -> 5.53 us
  matrix products: 20.4 us -> 0 us
  between operations: 14.2 us -> 0.84 us
  Pallas kernels: 0 us -> 8 us
    all_gather x1 -> x0, waiting for transfers between devices: 326 us -> none  [local(): gathered = lax.all_gather(features, ('team', 'row'), axis=0, tiled=True)]
    psum x1 -> x0, waiting for transfers between devices: 74.8 us -> none  [local(): summed = lax.psum((weight_part, bias_part), ('team', 'row'))]
    psum x1 -> x0, blocking collectives: 65.8 us -> none  [local(): summed = lax.psum((weight_part, bias_part), ('team', 'row'))]
    all_to_all x0 -> x1, waiting for transfers between devices: none -> 41.8 us  [local(): slices = lax.all_to_all(picked, PLANE, 0, 0)]
    ppermute x0 -> x18, starting transfers between devices: none -> 36.3 us  [the longest x9 25.3 us: ring(): lax.ppermute(value, axis, [(i, (i + step) % size) for i in range(size)])]
    dot_general x10 -> x0, matrix products: 20.4 us -> none  [the longest x4 13.1 us: local(): jnp.einsum('sij,sjf->sif', tiles, picked, preferred_element_type=jnp.floa...]
    ppermute x0 -> x18, waiting for transfers between devices: none -> 18.1 us  [the longest x9 10 us: ring(): return lax.ppermute(value, ('zlo', 'zhi'), pairs)]
    all_to_all x0 -> x1, blocking collectives: none -> 14.5 us  [local(): dealt = lax.all_to_all(jnp.concatenate([mine, lists], axis=1), PLANE, 0, 0)]
  transfers between devices with their start and end apart: 2 -> 19, of which waited for: 2 -> 16; matrix products, arithmetic and copies ran while one was open for 1% -> 0% of each run, Pallas kernels for 0% -> 0%
where the time goes in v1:
time: 132 us
  waiting for transfers between devices  59.9 us (45%)
  starting transfers between devices  40.2 us (30%)
  blocking collectives  14.5 us (11%)
  Pallas kernels  8 us (6%)
  local copies, waits for them, and re-layouts  5.53 us (4%)
  other arithmetic  2.88 us (2%)
    all_to_all x1, waiting for transfers between devices, local(): slices = lax.all_to_all(picked, PLANE, 0, 0)  41.8 us
    ppermute x9, starting transfers between devices, ring(): lax.ppermute(value, axis, [(i, (i + step) % size) for i in range(size)])  25.3 us
    all_to_all x1, blocking collectives, local(): dealt = lax.all_to_all(jnp.concatenate([mine, lists], axis=1), PLANE, 0, 0)  14.5 us
    ppermute x9, starting transfers between devices, ring(): return lax.ppermute(value, ('zlo', 'zhi'), pairs)  11.1 us
    ppermute x9, waiting for transfers between devices, ring(): return lax.ppermute(value, ('zlo', 'zhi'), pairs)  10 us
    ppermute x9, waiting for transfers between devices, ring(): lax.ppermute(value, axis, [(i, (i + step) % size) for i in range(size)])  8.1 us
    pallas_call x1, Pallas kernels, layer(): pl.pallas_call(layer_kernel, out_shape=(jax.ShapeDtypeStruct((nodes, out_...  4.74 us
    all_to_all x1, starting transfers between devices, local(): slices = lax.all_to_all(picked, PLANE, 0, 0)  3.88 us
  transfers between devices with their start and end apart: 19, of which 16 were waited for; matrix products, arithmetic and copies ran while one was open for 0% of the time, Pallas kernels for 0%

profile of v1, /device:TPU:1, one launch (start us, length us, event | category | flops | bytes accessed | tf_op | source)
XLA Modules:
  0.0 131.9 jit_solution(11024512351869798535)
XLA Ops:
  0.7 0.8 fusion.11
  1.4 0.1 reshape.85
  1.6 0.9 pad_maximum_fusion.1
  2.5 14.5 %all_to_all.10 = bf16[16,3,16,128]{3,2,1,0:T(8,128)(2,1)S(1)} all-to-all(bf16[16,3,16,128]{3,2,1,0:T(8,128)(2,1)S(1)} %copy.17), channel_id=1, replica_groups=mesh['zlo'=2,'core'=2,'x'=4,'zhi'=2,'y'=4] {'x','y'}, dimensions={0} | all-to-all | bytes 393216 | tf_op jit(solution)/shard_map/all_to_all | solution.py:187
  17.1 3.8 %collective-permute-start = (bf16[32,16,128]{2,1,0:T(8,128)(2,1)S(1)}, bf16[32,16,128]{2,1,0:T(8,128)(2,1)S(1)}, u32[]{:S(2)}, u32[]{:S(2)}) collective-permute-start(bf16[32,16,128]{2,1,0:T(8,128)(2,1)S(1)} %bitcast.44), channel_id=1, source_target_pairs={{0,68},{4,64},{64,0},{68,4},{1,69},{5,65},{65,1},{69,5},{2,70},{6,... | collective-permute-start | bytes 393224 | tf_op jit(solution)/shard_map/ppermute | solution.py:23
  20.9 0.7 collective-permute-start.2
  21.6 2.1 %collective-permute-done.one_ref = bf16[32,16,128]{2,1,0:T(8,128)(2,1)S(1)} collective-permute-done((bf16[32,16,128]{2,1,0:T(8,128)(2,1)S(1)}, bf16[32,16,128]{2,1,0:T(8,128)(2,1)S(1)}, u32[]{:S(2)}, u32[]{:S(2)}) %collective-permute-start) | collective-permute-done | bytes 131104 | tf_op jit(solution)/shard_map/ppermute | solution.py:23
  23.7 2.6 %collective-permute-done.1.two_ref = bf16[32,16,128]{2,1,0:T(8,128)(2,1)S(1)} collective-permute-done((bf16[32,16,128]{2,1,0:T(8,128)(2,1)S(1)}, bf16[32,16,128]{2,1,0:T(8,128)(2,1)S(1)}, u32[]{:S(2)}, u32[]{:S(2)}) %collective-permute-start.1) | collective-permute-done | bytes 131104 | tf_op jit(solution)/shard_map/ppermute | solution.py:23
  26.3 1.3 %collective-permute-done.2.three_ref = bf16[32,16,128]{2,1,0:T(8,128)(2,1)S(1)} collective-permute-done((bf16[32,16,128]{2,1,0:T(8,128)(2,1)S(1)}, bf16[32,16,128]{2,1,0:T(8,128)(2,1)S(1)}, u32[]{:S(2)}, u32[]{:S(2)}) %collective-permute-start.2) | collective-permute-done | bytes 131104 | tf_op jit(solution)/shard_map/ppermute | solution.py:23
  27.6 0.1 pad_maximum_fusion
  27.7 3.3 %collective-permute-start.3 = (bf16[128,16,128]{2,1,0:T(8,128)(2,1)S(1)}, bf16[128,16,128]{2,1,0:T(8,128)(2,1)S(1)}, u32[]{:S(2)}, u32[]{:S(2)}) collective-permute-start(bf16[128,16,128]{2,1,0:T(8,128)(2,1)S(1)} %pad_maximum_fusion), channel_id=1, source_target_pairs={{0,32},{32,0},{1,33},{33,1},{2,34},{34,2},{3,35},{35,3},{4,36},{36... | collective-permute-start | bytes 1572872 | tf_op jit(solution)/shard_map/ppermute | solution.py:25
  31.0 1.5 %collective-permute-done.3.other_ref = bf16[128,16,128]{2,1,0:T(8,128)(2,1)S(1)} collective-permute-done((bf16[128,16,128]{2,1,0:T(8,128)(2,1)S(1)}, bf16[128,16,128]{2,1,0:T(8,128)(2,1)S(1)}, u32[]{:S(2)}, u32[]{:S(2)}) %collective-permute-start.3) | collective-permute-done | bytes 524320 | tf_op jit(solution)/shard_map/ppermute | solution.py:25
  32.5 3.3 %pick_slices.1 = bf16[16,48,16,128]{3,2,1,0:T(8,128)(2,1)} custom-call(s32[16,48]{1,0:T(8,128)S(1)} %fusion.2.need_ref, bf16[32,16,128]{2,1,0:T(8,128)(2,1)S(1)} %bitcast.48, bf16[32,16,128]{2,1,0:T(8,128)(2,1)S(1)} %collective-permute-done.one_ref, bf16[32,16,128]{2,1,0:T(8,128)(2,1)S(1)} %collective-permute-done.1.two_ref, ...), custom_call_target="tpu_custom_call" | custom-call | tf_op jit(solution)/shard_map/pick_slices/pallas_call | solution.py:46
  35.8 3.9 %all-to-all-start.1 = ((bf16[16,48,16,128]{3,2,1,0:T(8,128)(2,1)}), bf16[16,48,16,128]{3,2,1,0:T(8,128)(2,1)S(1)}, u32[]{:S(2)}, u32[]{:S(2)}) async-start(bf16[16,48,16,128]{3,2,1,0:T(8,128)(2,1)} %pick_slices.1), calls=%async_computation.1 | async-start | bytes 6291456 | tf_op jit(solution)/shard_map/all_to_all | solution.py:195
  39.7 41.8 %all-to-all-done.1.slices_ref = bf16[16,48,16,128]{3,2,1,0:T(8,128)(2,1)S(1)} async-done(((bf16[16,48,16,128]{3,2,1,0:T(8,128)(2,1)}), bf16[16,48,16,128]{3,2,1,0:T(8,128)(2,1)S(1)}, u32[]{:S(2)}, u32[]{:S(2)}) %all-to-all-start.1) | async-done | bytes 3145760 | tf_op jit(solution)/shard_map/all_to_all | solution.py:195
  81.5 2.8 %copy-done = bf16[4,12,256,256]{3,2,1,0:T(8,128)(2,1)S(1)} copy-done((bf16[4,12,256,256]{3,2,1,0:T(8,128)(2,1)S(1)}, bf16[4,12,256,256]{3,2,1,0:T(8,128)(2,1)}, u32[]{:S(2)}) %copy-start) | copy-done | bytes 6291480
  84.3 4.7 %layer.1 = (bf16[512,256]{1,0:T(8,128)(2,1)}, f32[8,24,256]{2,1,0:T(8,128)S(1)}) custom-call(s32[4,12]{1,0:T(4,128)S(1)} %copy-done.4, s32[4]{0:T(128)S(1)} %copy-done.6, bf16[4,12,256,256]{3,2,1,0:T(8,128)(2,1)S(1)} %copy-done, bf16[16,48,16,128]{3,2,1,0:T(8,128)(2,1)S(1)} %all-to-all-done.1.slices_ref, bf16[128,256]{1,0:T(8,128)(2,1)S(1)} %copy-done.3, ...), custom_call_target="tpu_custom_call" | custom-call | tf_op jit(solution)/shard_map/layer/pallas_call | solution.py:116
  89.0 0.7 copy-done.2
  89.7 1.1 collective-permute-start.4
  90.8 0.9 collective-permute-done.4
  91.8 0.9 bitcast_add_fusion
  92.7 0.1 collective-permute-start.5
  92.8 2.0 %collective-permute-start.6 = (f32[24,256]{1,0:T(8,128)S(1)}, f32[24,256]{1,0:T(8,128)S(1)}, u32[]{:S(2)}, u32[]{:S(2)}) collective-permute-start(f32[24,256]{1,0:T(8,128)S(1)} %get-tuple-element.11), channel_id=1, source_target_pairs={{0,4},{4,0},{64,68},{68,64},{1,5},{5,1},{65,69},{69,65},{2,6},{6,2... | collective-permute-start | bytes 73736 | tf_op jit(solution)/shard_map/ppermute | solution.py:23
  94.8 0.8 collective-permute-start.7
  95.6 1.1 collective-permute-done.5
  96.7 0.4 collective-permute-done.6
  97.1 0.7 collective-permute-done.7
  97.8 9.0 %collective-permute-start.10 = (f32[24,256]{1,0:T(8,128)S(1)}, f32[24,256]{1,0:T(8,128)S(1)}, u32[]{:S(2)}, u32[]{:S(2)}) collective-permute-start(f32[24,256]{1,0:T(8,128)S(1)} %fusion.1), channel_id=1, source_target_pairs={{0,24},{8,0},{16,8},{24,16},{1,25},{9,1},{17,9},{25,17},{2,26},{10... | collective-permute-start | bytes 73736 | tf_op jit(solution)/shard_map/ppermute | solution.py:25
  106.8 0.7 collective-permute-start.9
  107.5 0.3 collective-permute-done.10
  107.7 3.2 %collective-permute-done.8 = f32[24,256]{1,0:T(8,128)S(1)} collective-permute-done((f32[24,256]{1,0:T(8,128)S(1)}, f32[24,256]{1,0:T(8,128)S(1)}, u32[]{:S(2)}, u32[]{:S(2)}) %collective-permute-start.8) | collective-permute-done | bytes 24608 | tf_op jit(solution)/shard_map/ppermute | solution.py:25
  111.0 0.8 collective-permute-start.11
  111.8 1.6 %collective-permute-start.12 = (f32[24,256]{1,0:T(8,128)S(1)}, f32[24,256]{1,0:T(8,128)S(1)}, u32[]{:S(2)}, u32[]{:S(2)}) collective-permute-start(f32[24,256]{1,0:T(8,128)S(1)} %add_add_fusion.1), channel_id=1, source_target_pairs={{0,1},{1,2},{2,3},{3,0},{4,5},{5,6},{6,7},{7,4},{8,9},{9,10},{10,1... | collective-permute-start | bytes 73736 | tf_op jit(solution)/shard_map/ppermute | solution.py:25
  113.4 2.3 %collective-permute-start.13 = (f32[24,256]{1,0:T(8,128)S(1)}, f32[24,256]{1,0:T(8,128)S(1)}, u32[]{:S(2)}, u32[]{:S(2)}) collective-permute-start(f32[24,256]{1,0:T(8,128)S(1)} %add_add_fusion.1), channel_id=1, source_target_pairs={{0,3},{1,0},{2,1},{3,2},{4,7},{5,4},{6,5},{7,6},{8,11},{9,8},{10,9... | collective-permute-start | bytes 73736 | tf_op jit(solution)/shard_map/ppermute | solution.py:25
  115.7 1.2 collective-permute-done.12
  116.9 0.1 collective-permute-start.14
  117.0 2.8 %collective-permute-start.15 = (f32[24,256]{1,0:T(8,128)S(1)}, f32[24,256]{1,0:T(8,128)S(1)}, u32[]{:S(2)}, u32[]{:S(2)}) collective-permute-start(f32[24,256]{1,0:T(8,128)S(1)} %add_add_fusion), channel_id=1, source_target_pairs={{0,4},{4,0},{64,68},{68,64},{1,5},{5,1},{65,69},{69,65},{2,6},{6,2... | collective-permute-start | bytes 73736 | tf_op jit(solution)/shard_map/ppermute | solution.py:23
  119.8 0.8 collective-permute-start.16
  120.6 0.1 broadcast_in_dim.15
  120.7 0.5 collective-permute-done.14
  121.2 0.1 collective-permute-done.15
  121.3 1.2 collective-permute-done.16
  122.5 6.5 %collective-permute-start.17 = (f32[4,24,256]{2,1,0:T(8,128)S(1)}, f32[4,24,256]{2,1,0:T(8,128)S(1)}, u32[]{:S(2)}, u32[]{:S(2)}) collective-permute-start(f32[4,24,256]{2,1,0:T(8,128)S(1)} %pad_maximum_fusion.3), channel_id=1, source_target_pairs={{0,32},{32,0},{1,33},{33,1},{2,34},{34,2},{3,35},{35,3},{4,36},{36... | collective-permute-start | bytes 294920 | tf_op jit(solution)/shard_map/ppermute | solution.py:25
  129.0 0.9 collective-permute-done.17
  130.0 0.6 gather_fusion
  130.6 0.1 bitcast_select_fusion
  130.7 0.7 slice.20
  131.3 0.6 slice.21
  (39 shorter events, 0.3 us)
Async XLA Ops:
  17.1 6.6 %collective-permute-start = (bf16[32,16,128]{2,1,0:T(8,128)(2,1)S(1)}, bf16[32,16,128]{2,1,0:T(8,128)(2,1)S(1)}, u32[]{:S(2)}, u32[]{:S(2)}) collective-permute-start(bf16[32,16,128]{2,1,0:T(8,128)(2,1)S(1)} %bitcast.44), channel_id=1, source_target_pairs={{0,68},{4,64},{64,0},{68,4},{1,69},{5,65},{65,1},{69,5},{2,70},{6,... | collective-permute-start | bytes 393224 | tf_op jit(solution)/shard_map/ppermute | solution.py:23
  20.9 5.4 %collective-permute-start.1 = (bf16[32,16,128]{2,1,0:T(8,128)(2,1)S(1)}, bf16[32,16,128]{2,1,0:T(8,128)(2,1)S(1)}, u32[]{:S(2)}, u32[]{:S(2)}) collective-permute-start(bf16[32,16,128]{2,1,0:T(8,128)(2,1)S(1)} %bitcast.45), channel_id=1, source_target_pairs={{0,4},{4,0},{64,68},{68,64},{1,5},{5,1},{65,69},{69,65},{2,6},{6,2... | collective-permute-start | bytes 393224 | tf_op jit(solution)/shard_map/ppermute | solution.py:23
  20.9 6.7 %collective-permute-start.2 = (bf16[32,16,128]{2,1,0:T(8,128)(2,1)S(1)}, bf16[32,16,128]{2,1,0:T(8,128)(2,1)S(1)}, u32[]{:S(2)}, u32[]{:S(2)}) collective-permute-start(bf16[32,16,128]{2,1,0:T(8,128)(2,1)S(1)} %bitcast.46), channel_id=1, source_target_pairs={{0,64},{4,68},{64,4},{68,0},{1,65},{5,69},{65,5},{69,1},{2,66},{6,... | collective-permute-start | bytes 393224 | tf_op jit(solution)/shard_map/ppermute | solution.py:23
  27.7 4.8 %collective-permute-start.3 = (bf16[128,16,128]{2,1,0:T(8,128)(2,1)S(1)}, bf16[128,16,128]{2,1,0:T(8,128)(2,1)S(1)}, u32[]{:S(2)}, u32[]{:S(2)}) collective-permute-start(bf16[128,16,128]{2,1,0:T(8,128)(2,1)S(1)} %pad_maximum_fusion), channel_id=1, source_target_pairs={{0,32},{32,0},{1,33},{33,1},{2,34},{34,2},{3,35},{35,3},{4,36},{36... | collective-permute-start | bytes 1572872 | tf_op jit(solution)/shard_map/ppermute | solution.py:25
  35.8 45.7 %copy-start.1 = (bf16[512,256]{1,0:T(8,128)(2,1)S(1)}, bf16[512,256]{1,0:T(8,128)(2,1)}, u32[]{:S(2)}) copy-start(bf16[512,256]{1,0:T(8,128)(2,1)} %cotangent_ref.1) | copy-start | bytes 786436
  35.8 45.7 %copy-start.3 = (bf16[128,256]{1,0:T(8,128)(2,1)S(1)}, bf16[128,256]{1,0:T(8,128)(2,1)}, u32[]{:S(2)}) copy-start(bf16[128,256]{1,0:T(8,128)(2,1)} %weight_ref.1) | copy-start | bytes 196612
  35.8 45.7 %copy-start.4 = (s32[4,12]{1,0:T(4,128)S(1)}, s32[4,12]{1,0:T(4,128)}, u32[]{:S(2)}) copy-start(s32[4,12]{1,0:T(4,128)} %row_ref.1) | copy-start | bytes 580
  35.8 45.7 %copy-start.5 = (f32[256]{0:T(256)S(1)}, f32[256]{0:T(256)}, u32[]{:S(2)}) copy-start(f32[256]{0:T(256)} %param.14) | copy-start | bytes 3076
  35.8 45.7 %copy-start.6 = (s32[4]{0:T(128)S(1)}, s32[4]{0:T(128)}, u32[]{:S(2)}) copy-start(s32[4]{0:T(128)} %count_ref.1) | copy-start | bytes 52
  35.8 45.7 %all-to-all-start.1 = ((bf16[16,48,16,128]{3,2,1,0:T(8,128)(2,1)}), bf16[16,48,16,128]{3,2,1,0:T(8,128)(2,1)S(1)}, u32[]{:S(2)}, u32[]{:S(2)}) async-start(bf16[16,48,16,128]{3,2,1,0:T(8,128)(2,1)} %pick_slices.1), calls=%async_computation.1 | async-start | bytes 6291456 | tf_op jit(solution)/shard_map/all_to_all | solution.py:195
  81.5 2.8 %copy-start = (bf16[4,12,256,256]{3,2,1,0:T(8,128)(2,1)S(1)}, bf16[4,12,256,256]{3,2,1,0:T(8,128)(2,1)}, u32[]{:S(2)}) copy-start(bf16[4,12,256,256]{3,2,1,0:T(8,128)(2,1)} %tiles_ref.1) | copy-start | bytes 18874372
  89.0 0.7 copy-start.2
  89.7 2.1 %collective-permute-start.4 = (f32[4,24,256]{2,1,0:T(8,128)S(1)}, f32[4,24,256]{2,1,0:T(8,128)S(1)}, u32[]{:S(2)}, u32[]{:S(2)}) collective-permute-start(f32[4,24,256]{2,1,0:T(8,128)S(1)} %dynamic-slice_bitcast_fusion), channel_id=1, source_target_pairs={{0,32},{32,0},{1,33},{33,1},{2,34},{34,2},{3,35},{35,3},{4,36},{36... | collective-permute-start | bytes 294920 | tf_op jit(solution)/shard_map/ppermute | solution.py:25
  92.7 4.0 %collective-permute-start.5 = (f32[24,256]{1,0:T(8,128)S(1)}, f32[24,256]{1,0:T(8,128)S(1)}, u32[]{:S(2)}, u32[]{:S(2)}) collective-permute-start(f32[24,256]{1,0:T(8,128)S(1)} %get-tuple-element.9), channel_id=1, source_target_pairs={{0,64},{4,68},{64,4},{68,0},{1,65},{5,69},{65,5},{69,1},{2,66},{6,... | collective-permute-start | bytes 73736 | tf_op jit(solution)/shard_map/ppermute | solution.py:23
  92.8 4.3 %collective-permute-start.6 = (f32[24,256]{1,0:T(8,128)S(1)}, f32[24,256]{1,0:T(8,128)S(1)}, u32[]{:S(2)}, u32[]{:S(2)}) collective-permute-start(f32[24,256]{1,0:T(8,128)S(1)} %get-tuple-element.11), channel_id=1, source_target_pairs={{0,4},{4,0},{64,68},{68,64},{1,5},{5,1},{65,69},{69,65},{2,6},{6,2... | collective-permute-start | bytes 73736 | tf_op jit(solution)/shard_map/ppermute | solution.py:23
  94.8 3.0 %collective-permute-start.7 = (f32[24,256]{1,0:T(8,128)S(1)}, f32[24,256]{1,0:T(8,128)S(1)}, u32[]{:S(2)}, u32[]{:S(2)}) collective-permute-start(f32[24,256]{1,0:T(8,128)S(1)} %get-tuple-element.10), channel_id=1, source_target_pairs={{0,68},{4,64},{64,0},{68,4},{1,69},{5,65},{65,1},{69,5},{2,70},{6,... | collective-permute-start | bytes 73736 | tf_op jit(solution)/shard_map/ppermute | solution.py:23
  97.8 9.9 %collective-permute-start.10 = (f32[24,256]{1,0:T(8,128)S(1)}, f32[24,256]{1,0:T(8,128)S(1)}, u32[]{:S(2)}, u32[]{:S(2)}) collective-permute-start(f32[24,256]{1,0:T(8,128)S(1)} %fusion.1), channel_id=1, source_target_pairs={{0,24},{8,0},{16,8},{24,16},{1,25},{9,1},{17,9},{25,17},{2,26},{10... | collective-permute-start | bytes 73736 | tf_op jit(solution)/shard_map/ppermute | solution.py:25
  106.8 4.2 %collective-permute-start.8 = (f32[24,256]{1,0:T(8,128)S(1)}, f32[24,256]{1,0:T(8,128)S(1)}, u32[]{:S(2)}, u32[]{:S(2)}) collective-permute-start(f32[24,256]{1,0:T(8,128)S(1)} %fusion.1), channel_id=1, source_target_pairs={{0,16},{8,24},{16,0},{24,8},{1,17},{9,25},{17,1},{25,9},{2,18},{10... | collective-permute-start | bytes 73736 | tf_op jit(solution)/shard_map/ppermute | solution.py:25
  106.8 4.2 %collective-permute-start.9 = (f32[24,256]{1,0:T(8,128)S(1)}, f32[24,256]{1,0:T(8,128)S(1)}, u32[]{:S(2)}, u32[]{:S(2)}) collective-permute-start(f32[24,256]{1,0:T(8,128)S(1)} %fusion.1), channel_id=1, source_target_pairs={{0,8},{8,16},{16,24},{24,0},{1,9},{9,17},{17,25},{25,1},{2,10},{10... | collective-permute-start | bytes 73736 | tf_op jit(solution)/shard_map/ppermute | solution.py:25
  111.0 4.7 %collective-permute-start.11 = (f32[24,256]{1,0:T(8,128)S(1)}, f32[24,256]{1,0:T(8,128)S(1)}, u32[]{:S(2)}, u32[]{:S(2)}) collective-permute-start(f32[24,256]{1,0:T(8,128)S(1)} %add_add_fusion.1), channel_id=1, source_target_pairs={{0,2},{1,3},{2,0},{3,1},{4,6},{5,7},{6,4},{7,5},{8,10},{9,11},{10,... | collective-permute-start | bytes 73736 | tf_op jit(solution)/shard_map/ppermute | solution.py:25
  111.8 5.2 %collective-permute-start.12 = (f32[24,256]{1,0:T(8,128)S(1)}, f32[24,256]{1,0:T(8,128)S(1)}, u32[]{:S(2)}, u32[]{:S(2)}) collective-permute-start(f32[24,256]{1,0:T(8,128)S(1)} %add_add_fusion.1), channel_id=1, source_target_pairs={{0,1},{1,2},{2,3},{3,0},{4,5},{5,6},{6,7},{7,4},{8,9},{9,10},{10,1... | collective-permute-start | bytes 73736 | tf_op jit(solution)/shard_map/ppermute | solution.py:25
  113.4 3.5 %collective-permute-start.13 = (f32[24,256]{1,0:T(8,128)S(1)}, f32[24,256]{1,0:T(8,128)S(1)}, u32[]{:S(2)}, u32[]{:S(2)}) collective-permute-start(f32[24,256]{1,0:T(8,128)S(1)} %add_add_fusion.1), channel_id=1, source_target_pairs={{0,3},{1,0},{2,1},{3,2},{4,7},{5,4},{6,5},{7,6},{8,11},{9,8},{10,9... | collective-permute-start | bytes 73736 | tf_op jit(solution)/shard_map/ppermute | solution.py:25
  116.9 4.2 %collective-permute-start.14 = (f32[24,256]{1,0:T(8,128)S(1)}, f32[24,256]{1,0:T(8,128)S(1)}, u32[]{:S(2)}, u32[]{:S(2)}) collective-permute-start(f32[24,256]{1,0:T(8,128)S(1)} %add_add_fusion), channel_id=1, source_target_pairs={{0,64},{4,68},{64,4},{68,0},{1,65},{5,69},{65,5},{69,1},{2,66},{6,... | collective-permute-start | bytes 73736 | tf_op jit(solution)/shard_map/ppermute | solution.py:23
  117.0 4.3 %collective-permute-start.15 = (f32[24,256]{1,0:T(8,128)S(1)}, f32[24,256]{1,0:T(8,128)S(1)}, u32[]{:S(2)}, u32[]{:S(2)}) collective-permute-start(f32[24,256]{1,0:T(8,128)S(1)} %add_add_fusion), channel_id=1, source_target_pairs={{0,4},{4,0},{64,68},{68,64},{1,5},{5,1},{65,69},{69,65},{2,6},{6,2... | collective-permute-start | bytes 73736 | tf_op jit(solution)/shard_map/ppermute | solution.py:23
  119.8 2.7 %collective-permute-start.16 = (f32[24,256]{1,0:T(8,128)S(1)}, f32[24,256]{1,0:T(8,128)S(1)}, u32[]{:S(2)}, u32[]{:S(2)}) collective-permute-start(f32[24,256]{1,0:T(8,128)S(1)} %add_add_fusion), channel_id=1, source_target_pairs={{0,68},{4,64},{64,0},{68,4},{1,69},{5,65},{65,1},{69,5},{2,70},{6,... | collective-permute-start | bytes 73736 | tf_op jit(solution)/shard_map/ppermute | solution.py:23
  122.5 7.4 %collective-permute-start.17 = (f32[4,24,256]{2,1,0:T(8,128)S(1)}, f32[4,24,256]{2,1,0:T(8,128)S(1)}, u32[]{:S(2)}, u32[]{:S(2)}) collective-permute-start(f32[4,24,256]{2,1,0:T(8,128)S(1)} %pad_maximum_fusion.3), channel_id=1, source_target_pairs={{0,32},{32,0},{1,33},{33,1},{2,34},{34,2},{3,35},{35,3},{4,36},{36... | collective-permute-start | bytes 294920 | tf_op jit(solution)/shard_map/ppermute | solution.py:25

commit v2 on v1

v2 whole, which is shorter than its diff:
```python
import jax
import jax.numpy as jnp
from jax import lax
from jax.experimental import pallas as pl
from jax.experimental.pallas import tpu as pltpu
from jax.sharding import Mesh, PartitionSpec as P

AXES = ("zlo", "core", "x", "zhi", "y")
AXIS_SIZES = (2, 2, 4, 2, 4)
PLANE = ("x", "y")
PEERS = 16


def z_of(index):
    return (index % 2) * 2 + index // 2


def ring(value, axis, step):
    if axis == "z":
        pairs = [(i, z_of((z_of(i) + step) % 4)) for i in range(4)]
        return lax.ppermute(value, ("zlo", "zhi"), pairs)
    size = lax.axis_size(axis)
    return lax.ppermute(value, axis, [(i, (i + step) % size) for i in range(size)])


def gather_kernel(need_ref, own_ref, one_ref, two_ref, three_ref, other_ref, out_ref, table_ref, stage_ref, sent):
    part = own_ref.shape[0]
    for at, piece in enumerate((own_ref, one_ref, two_ref, three_ref)):
        table_ref[at * part : (at + 1) * part] = piece[...]
    table_ref[4 * part :] = other_ref[...]
    slots = out_ref.shape[1]

    def one_peer(peer, carry):
        for slot in range(slots):
            stage_ref[peer, slot] = table_ref[need_ref[peer, slot]]
        return carry

    copies = []
    for run in range(sent.shape[0]):
        span = PEERS // sent.shape[0]
        lax.fori_loop(run * span, (run + 1) * span, one_peer, 0)
        peers = pl.ds(run * span, span)
        copies.append(pltpu.make_async_copy(stage_ref.at[peers], out_ref.at[peers], sent.at[run]))
        copies[-1].start()
    for copy in copies:
        copy.wait()


def gather_slices(need, own, one, two, three, other, slots):
    part, height, width = own.shape
    vmem = pl.BlockSpec(memory_space=pltpu.VMEM)
    shape = (PEERS, slots, height, width)
    return pl.pallas_call(
        gather_kernel,
        out_shape=jax.ShapeDtypeStruct(shape, own.dtype),
        in_specs=[pl.BlockSpec(memory_space=pltpu.SMEM)] + [vmem] * 5,
        out_specs=pl.BlockSpec(memory_space=pltpu.HBM),
        scratch_shapes=[
            pltpu.VMEM((8 * part, height, width), own.dtype),
            pltpu.VMEM(shape, own.dtype),
            pltpu.SemaphoreType.DMA((4,)),
        ],
        compiler_params=pltpu.CompilerParams(vmem_limit_bytes=24 * 1024 * 1024),
        name="pick_slices",
    )(need, own, one, two, three, other)


def gelu_parts(values):
    gelu_coef = 0.7978845608
    tangent_h = jnp.tanh(gelu_coef * (values + 0.044715 * values * values * values))
    result = 0.5 * values * (1.0 + tangent_h)
    derive = 0.5 * (1.0 + tangent_h) + 0.5 * values * (1.0 - tangent_h * tangent_h) * gelu_coef * (
        1.0 + 3.0 * 0.044715 * values * values
    )
    return (result, derive)


def layer_kernel(
    row_ref, count_ref, tiles_ref, slices_ref, weight_ref, bias_ref, cotangent_ref, hidden_ref, grad_ref, held, landed
):
    groups, slots = held.shape[:2]
    runs = landed.shape[1]
    span = slots // runs
    copies = []
    for group in range(groups):
        for run in range(runs):
            part = pl.ds(run * span, span)
            copies.append(
                pltpu.make_async_copy(tiles_ref.at[group, part], held.at[group, part], landed.at[group, run])
            )
            copies[-1].start()

    def spread(group, slot):
        picked = jnp.concatenate([slices_ref[i, group * slots + slot] for i in range(PEERS)], axis=0)
        row = jnp.where(slot < count_ref[group], row_ref[group, slot], 2)
        none = jnp.zeros_like(picked)
        return jnp.concatenate([jnp.where(row == 0, picked, none), jnp.where(row == 1, picked, none)], axis=1)

    total = None
    for group in range(groups):
        for run in range(runs):
            copies[group * runs + run].wait()
            part = range(run * span, (run + 1) * span)
            tiles = jnp.concatenate([held[group, slot] for slot in part], axis=1)
            picked = jnp.concatenate([spread(group, slot) for slot in part], axis=0)
            product = jnp.dot(tiles, picked, preferred_element_type=jnp.float32)
            total = product if total is None else total + product

    width = total.shape[1] // 2
    aggregated = jnp.concatenate([total[:, :width], total[:, width:]], axis=0).astype(jnp.bfloat16)
    pre = jnp.dot(aggregated, weight_ref[...], preferred_element_type=jnp.float32) + bias_ref[...]
    result, derive = gelu_parts(pre)
    hidden_ref[...] = result.astype(jnp.bfloat16)
    slope = cotangent_ref[...].astype(jnp.float32) * derive
    outs = slope.shape[1]
    grad_ref[:, :outs] = lax.dot_general(
        aggregated, slope.astype(jnp.bfloat16), (((0,), (0,)), ((), ())), preferred_element_type=jnp.float32
    )
    bias_part = jnp.sum(slope, axis=0, keepdims=True)
    at = lax.broadcasted_iota(jnp.int32, (width, outs - width), 0)
    last = jnp.where(at == 1, bias_part[:, width:], 0.0)
    grad_ref[:, outs:] = jnp.where(at == 0, bias_part[:, :width], last)


def layer(rows, counts, tiles, slices, weight, bias, cotangent):
    nodes, out_width = cotangent.shape
    width = weight.shape[0]
    runs = 2
    vmem = pl.BlockSpec(memory_space=pltpu.VMEM)
    smem = pl.BlockSpec(memory_space=pltpu.SMEM)
    return pl.pallas_call(
        layer_kernel,
        out_shape=(
            jax.ShapeDtypeStruct((nodes, out_width), jnp.bfloat16),
            jax.ShapeDtypeStruct((width, out_width + width), jnp.float32),
        ),
        in_specs=[smem, smem, pl.BlockSpec(memory_space=pltpu.HBM), vmem, vmem, vmem, vmem],
        out_specs=(vmem, vmem),
        scratch_shapes=[
            pltpu.VMEM(tiles.shape, tiles.dtype),
            pltpu.SemaphoreType.DMA((tiles.shape[0], runs)),
        ],
        compiler_params=pltpu.CompilerParams(vmem_limit_bytes=32 * 1024 * 1024),
        name="layer",
    )(rows, counts, tiles, slices, weight, bias.reshape(1, -1), cotangent)


def sum_over_devices(grad):
    rows = grad.reshape(grad.shape[0], -1, 128)
    total = jnp.sum(lax.all_to_all(rows, AXES, 0, 0), axis=0)
    return lax.all_to_all(jnp.broadcast_to(total[None], rows.shape), AXES, 0, 0)


def local(features, tile_values, tile_row, tile_col, tile_count, weight, bias, cotangent):
    groups, slots, block, _ = tile_values.shape
    width = features.shape[1]
    height = block // PEERS
    needed = groups * slots
    core = lax.axis_index("core")
    depth = lax.axis_index("zhi") * 2 + lax.axis_index("zlo")

    team = lax.broadcasted_iota(jnp.int32, (groups, slots), 0)
    holder, part = tile_col // 2, tile_col % 2
    there = ((holder // 4) % 2) * 2 + team // 2
    place = ((holder // 8) * 4 + holder % 4) * 2 + part
    turn = (team % 2) ^ core
    need = ((turn * 4 + (there - depth) % 4) * (2 * PEERS) + place).astype(jnp.bfloat16).reshape(1, needed)
    need = jnp.broadcast_to(jnp.pad(need, ((0, 0), (0, width - needed))), (height, width))

    mine = features.reshape(-1, PEERS, height, width).transpose(1, 0, 2, 3)
    lists = jnp.broadcast_to(need[None, None], (PEERS, 1, height, width))
    dealt = lax.all_to_all(jnp.concatenate([mine, lists], axis=1), PLANE, 0, 0)
    own = dealt[:, :2].reshape(2 * PEERS, height, width)
    wanted = dealt[:, 2, 0, :needed].astype(jnp.int32)

    one, two, three = (ring(own, "z", -step) for step in (1, 2, 3))
    other = ring(jnp.concatenate([own, one, two, three], axis=0), "core", 1)

    picked = gather_slices(wanted, own, one, two, three, other, needed)
    slices = lax.all_to_all(picked, PLANE, 0, 0)

    hidden, grad = layer(tile_row, tile_count, tile_values, slices, weight, bias, cotangent)
    summed = sum_over_devices(grad)
    return (hidden, summed[:, :2].reshape(weight.shape), summed[:2, 2].reshape(bias.shape))


def solution(mesh):
    fine = Mesh(mesh.devices.reshape(AXIS_SIZES), AXES)
    nodes = P(AXES)
    in_specs = (nodes, nodes, nodes, nodes, nodes, P(), P(), nodes)
    return jax.shard_map(
        local, mesh=fine, in_specs=in_specs, out_specs=(nodes, P(), P()), check_vma=False
    )
```

time: 132 us -> 116 us (0.88)
  blocking collectives: 14.5 us -> 89.7 us
  waiting for transfers between devices: 59.9 us -> 5.81 us
  starting transfers between devices: 40.2 us -> 8.29 us
  local copies, waits for them, and re-layouts: 5.53 us -> 1.78 us
    all_to_all x0 -> x3, blocking collectives: none -> 75 us  [the longest x1 41.7 us: local(): slices = lax.all_to_all(picked, PLANE, 0, 0)]
    all_to_all x1 -> x0, waiting for transfers between devices: 41.8 us -> none  [local(): slices = lax.all_to_all(picked, PLANE, 0, 0)]
    ppermute x9 -> x1, starting transfers between devices: 25.3 us -> 2.55 us  [ring(): lax.ppermute(value, axis, [(i, (i + step) % size) for i in range(size)])]
    ppermute x9 -> x1, waiting for transfers between devices: 8.1 us -> 1.5 us  [ring(): lax.ppermute(value, axis, [(i, (i + step) % size) for i in range(size)])]
    ppermute x9 -> x3, waiting for transfers between devices: 10 us -> 4.31 us  [ring(): return lax.ppermute(value, ('zlo', 'zhi'), pairs)]
    ppermute x9 -> x3, starting transfers between devices: 11.1 us -> 5.74 us  [ring(): return lax.ppermute(value, ('zlo', 'zhi'), pairs)]
    all_to_all x1 -> x0, starting transfers between devices: 3.88 us -> none  [local(): slices = lax.all_to_all(picked, PLANE, 0, 0)]
    unnamed x14 -> x15, local copies, waits for them, and re-layouts: 3.48 us -> 0.71 us
  transfers between devices with their start and end apart: 19 -> 4, of which waited for: 16 -> 4; matrix products, arithmetic and copies ran while one was open for 0% -> 0% of each run, Pallas kernels for 0% -> 0%
where the time goes in v2:
time: 116 us
  blocking collectives  89.7 us (77%)
  starting transfers between devices  8.29 us (7%)
  Pallas kernels  7.86 us (7%)
  waiting for transfers between devices  5.81 us (5%)
  other arithmetic  1.93 us (2%)
  local copies, waits for them, and re-layouts  1.78 us (2%)
    all_to_all x1, blocking collectives, local(): slices = lax.all_to_all(picked, PLANE, 0, 0)  41.7 us
    all_to_all x1, blocking collectives, sum_over_devices(): total = jnp.sum(lax.all_to_all(rows, AXES, 0, 0), axis=0)  18 us
    all_to_all x1, blocking collectives, sum_over_devices(): return lax.all_to_all(jnp.broadcast_to(total[None], rows.shape), AXES, 0, 0)  15.3 us
    all_to_all x1, blocking collectives, local(): dealt = lax.all_to_all(jnp.concatenate([mine, lists], axis=1), PLANE, 0, 0)  14.8 us
    pallas_call x1, Pallas kernels, layer(): pl.pallas_call(layer_kernel, out_shape=(jax.ShapeDtypeStruct((nodes, out_...  5.98 us
    ppermute x3, starting transfers between devices, ring(): return lax.ppermute(value, ('zlo', 'zhi'), pairs)  5.74 us
    ppermute x3, waiting for transfers between devices, ring(): return lax.ppermute(value, ('zlo', 'zhi'), pairs)  4.31 us
    ppermute x1, starting transfers between devices, ring(): lax.ppermute(value, axis, [(i, (i + step) % size) for i in range(size)])  2.55 us
  transfers between devices with their start and end apart: 4, of which 4 were waited for; matrix products, arithmetic and copies ran while one was open for 0% of the time, Pallas kernels for 0%

profile of v2, /device:TPU:1, one launch (start us, length us, event | category | flops | bytes accessed | tf_op | source)
XLA Modules:
  0.0 116.3 jit_solution(6865593544973620421)
XLA Ops:
  0.7 0.8 fusion.9
  1.4 0.1 reshape.29
  1.6 0.9 pad_maximum_fusion.1
  2.5 0.0 slice-start
  2.5 14.8 %all_to_all.20 = bf16[16,3,16,128]{3,2,1,0:T(8,128)(2,1)S(1)} all-to-all(bf16[16,3,16,128]{3,2,1,0:T(8,128)(2,1)S(1)} %copy.15), channel_id=1, replica_groups=mesh['zlo'=2,'core'=2,'x'=4,'zhi'=2,'y'=4] {'x','y'}, dimensions={0} | all-to-all | bytes 393216 | tf_op jit(solution)/shard_map/all_to_all | solution.py:172
  17.3 1.7 %collective-permute-start.2 = (bf16[32,16,128]{2,1,0:T(8,128)(2,1)S(1)}, bf16[32,16,128]{2,1,0:T(8,128)(2,1)S(1)}, u32[]{:S(2)}, u32[]{:S(2)}) collective-permute-start(bf16[32,16,128]{2,1,0:T(8,128)(2,1)S(1)} %bitcast.20), channel_id=1, source_target_pairs={{0,64},{4,68},{64,4},{68,0},{1,65},{5,69},{65,5},{69,1},{2,66},{6,... | collective-permute-start | bytes 393224 | tf_op jit(solution)/shard_map/ppermute | solution.py:21
  19.0 3.3 %collective-permute-start.1 = (bf16[32,16,128]{2,1,0:T(8,128)(2,1)S(1)}, bf16[32,16,128]{2,1,0:T(8,128)(2,1)S(1)}, u32[]{:S(2)}, u32[]{:S(2)}) collective-permute-start(bf16[32,16,128]{2,1,0:T(8,128)(2,1)S(1)} %bitcast.21), channel_id=1, source_target_pairs={{0,4},{4,0},{64,68},{68,64},{1,5},{5,1},{65,69},{69,65},{2,6},{6,2... | collective-permute-start | bytes 393224 | tf_op jit(solution)/shard_map/ppermute | solution.py:21
  22.3 0.7 collective-permute-start
  23.1 0.4 collective-permute-done.2.three_ref
  23.5 3.0 %collective-permute-done.1.two_ref = bf16[32,16,128]{2,1,0:T(8,128)(2,1)S(1)} collective-permute-done((bf16[32,16,128]{2,1,0:T(8,128)(2,1)S(1)}, bf16[32,16,128]{2,1,0:T(8,128)(2,1)S(1)}, u32[]{:S(2)}, u32[]{:S(2)}) %collective-permute-start.1) | collective-permute-done | bytes 131104 | tf_op jit(solution)/shard_map/ppermute | solution.py:21
  26.5 0.9 collective-permute-done.one_ref
  27.4 0.1 pad_maximum_fusion
  27.5 2.6 %collective-permute-start.3 = (bf16[128,16,128]{2,1,0:T(8,128)(2,1)S(1)}, bf16[128,16,128]{2,1,0:T(8,128)(2,1)S(1)}, u32[]{:S(2)}, u32[]{:S(2)}) collective-permute-start(bf16[128,16,128]{2,1,0:T(8,128)(2,1)S(1)} %pad_maximum_fusion), channel_id=1, source_target_pairs={{0,32},{32,0},{1,33},{33,1},{2,34},{34,2},{3,35},{35,3},{4,36},{36... | collective-permute-start | bytes 1572872 | tf_op jit(solution)/shard_map/ppermute | solution.py:23
  30.0 0.0 slice-start.1
  30.0 1.5 %collective-permute-done.3.other_ref = bf16[128,16,128]{2,1,0:T(8,128)(2,1)S(1)} collective-permute-done((bf16[128,16,128]{2,1,0:T(8,128)(2,1)S(1)}, bf16[128,16,128]{2,1,0:T(8,128)(2,1)S(1)}, u32[]{:S(2)}, u32[]{:S(2)}) %collective-permute-start.3) | collective-permute-done | bytes 524320 | tf_op jit(solution)/shard_map/ppermute | solution.py:23
  31.5 1.9 %pick_slices.1 = bf16[16,48,16,128]{3,2,1,0:T(8,128)(2,1)S(1)} custom-call(s32[16,48]{1,0:T(8,128)S(1)} %fusion.need_ref, bf16[32,16,128]{2,1,0:T(8,128)(2,1)S(1)} %bitcast.24, bf16[32,16,128]{2,1,0:T(8,128)(2,1)S(1)} %collective-permute-done.one_ref, bf16[32,16,128]{2,1,0:T(8,128)(2,1)S(1)} %collective-permute-done.1.two_ref, ...), custom_call_target="tpu_custom_call" | custom-call | tf_op jit(solution)/shard_map/pick_slices/pallas_call | solution.py:53
  33.4 0.0 copy-start
  33.4 0.0 copy-start.1
  33.5 0.0 copy-start.2
  33.5 0.0 copy-start.3
  33.5 0.0 copy-start.4
  33.5 41.7 %all_to_all.21.slices_ref = bf16[16,48,16,128]{3,2,1,0:T(8,128)(2,1)S(1)} all-to-all(bf16[16,48,16,128]{3,2,1,0:T(8,128)(2,1)S(1)} %pick_slices.1), channel_id=1, replica_groups=mesh['zlo'=2,'core'=2,'x'=4,'zhi'=2,'y'=4] {'x','y'}, dimensions={0} | all-to-all | bytes 6291456 | tf_op jit(solution)/shard_map/all_to_all | solution.py:180
  75.2 0.0 slice-done
  75.2 0.0 slice-done.1
  75.2 0.0 copy-done
  75.2 0.0 copy-done.1
  75.2 0.0 copy-done.2
  75.2 0.0 copy-done.3
  75.3 0.0 copy-done.4
  75.3 6.0 %layer.1 = (bf16[512,256]{1,0:T(8,128)(2,1)}, f32[128,384]{1,0:T(8,128)S(1)}) custom-call(s32[4,12]{1,0:T(4,128)S(1)} %copy-done.2, s32[4]{0:T(128)S(1)} %copy-done.4, bf16[4,12,256,256]{3,2,1,0:T(8,128)(2,1)S(1)} %bitcast.19, bf16[16,48,16,128]{3,2,1,0:T(8,128)(2,1)S(1)} %all_to_all.21.slices_ref, bf16[128,256]{1,0:T(8,128)(2,1)S(1)} %copy-done.1, ...), custom_call_target="tpu_custom_call" | custom-call | tf_op jit(solution)/shard_map/layer/pallas_call | solution.py:131
  81.3 0.1 copy.17
  81.4 0.2 copy.18
  81.5 18.0 %all_to_all.22 = f32[128,3,128]{2,1,0:T(4,128)S(1)} all-to-all(f32[128,3,128]{2,1,0:T(4,128)S(1)} %copy.18), channel_id=1, replica_groups=mesh['zlo'=2,'core'=2,'x'=4,'zhi'=2,'y'=4] {'zlo','core','x','zhi','y'}, dimensions={0} | all-to-all | bytes 393216 | tf_op jit(solution)/shard_map/all_to_all | solution.py:150
  99.5 0.1 reduce_sum.9
  99.7 15.3 %all_to_all.23 = f32[128,3,128]{2,1,0:T(4,128)S(1)} all-to-all(f32[128,3,128]{2,1,0:T(4,128)S(1)} %broadcast_in_dim.2), channel_id=1, replica_groups=mesh['zlo'=2,'core'=2,'x'=4,'zhi'=2,'y'=4] {'zlo','core','x','zhi','y'}, dimensions={0} | all-to-all | bytes 393216 | tf_op jit(solution)/shard_map/all_to_all | solution.py:151
  115.0 0.7 copy.25
  115.7 0.6 slice.19
  (12 shorter events, 0.2 us)
Async XLA Ops:
  2.5 72.7 %slice-start = ((s8[6291456]{0:T(1024)(128)(4,1)}), s8[4194304]{0:T(1024)(128)(4,1)S(1)}, s32[]{:S(2)}) async-start(s8[6291456]{0:T(1024)(128)(4,1)} %bitcast.18), calls=%async_computation.4 | async-start | bytes 8388608
  17.3 6.2 %collective-permute-start.2 = (bf16[32,16,128]{2,1,0:T(8,128)(2,1)S(1)}, bf16[32,16,128]{2,1,0:T(8,128)(2,1)S(1)}, u32[]{:S(2)}, u32[]{:S(2)}) collective-permute-start(bf16[32,16,128]{2,1,0:T(8,128)(2,1)S(1)} %bitcast.20), channel_id=1, source_target_pairs={{0,64},{4,68},{64,4},{68,0},{1,65},{5,69},{65,5},{69,1},{2,66},{6,... | collective-permute-start | bytes 393224 | tf_op jit(solution)/shard_map/ppermute | solution.py:21
  19.0 7.5 %collective-permute-start.1 = (bf16[32,16,128]{2,1,0:T(8,128)(2,1)S(1)}, bf16[32,16,128]{2,1,0:T(8,128)(2,1)S(1)}, u32[]{:S(2)}, u32[]{:S(2)}) collective-permute-start(bf16[32,16,128]{2,1,0:T(8,128)(2,1)S(1)} %bitcast.21), channel_id=1, source_target_pairs={{0,4},{4,0},{64,68},{68,64},{1,5},{5,1},{65,69},{69,65},{2,6},{6,2... | collective-permute-start | bytes 393224 | tf_op jit(solution)/shard_map/ppermute | solution.py:21
  22.3 5.0 %collective-permute-start = (bf16[32,16,128]{2,1,0:T(8,128)(2,1)S(1)}, bf16[32,16,128]{2,1,0:T(8,128)(2,1)S(1)}, u32[]{:S(2)}, u32[]{:S(2)}) collective-permute-start(bf16[32,16,128]{2,1,0:T(8,128)(2,1)S(1)} %bitcast.22), channel_id=1, source_target_pairs={{0,68},{4,64},{64,0},{68,4},{1,69},{5,65},{65,1},{69,5},{2,70},{6,... | collective-permute-start | bytes 393224 | tf_op jit(solution)/shard_map/ppermute | solution.py:21
  27.5 4.1 %collective-permute-start.3 = (bf16[128,16,128]{2,1,0:T(8,128)(2,1)S(1)}, bf16[128,16,128]{2,1,0:T(8,128)(2,1)S(1)}, u32[]{:S(2)}, u32[]{:S(2)}) collective-permute-start(bf16[128,16,128]{2,1,0:T(8,128)(2,1)S(1)} %pad_maximum_fusion), channel_id=1, source_target_pairs={{0,32},{32,0},{1,33},{33,1},{2,34},{34,2},{3,35},{35,3},{4,36},{36... | collective-permute-start | bytes 1572872 | tf_op jit(solution)/shard_map/ppermute | solution.py:23
  30.0 45.2 %slice-start.1 = ((s8[6291456]{0:T(1024)(128)(4,1)}), s8[2097152]{0:T(1024)(128)(4,1)S(1)}, s32[]{:S(2)}) async-start(s8[6291456]{0:T(1024)(128)(4,1)} %bitcast.18), calls=%async_computation.5 | async-start | bytes 4194304
  33.4 41.8 %copy-start = (bf16[512,256]{1,0:T(8,128)(2,1)S(1)}, bf16[512,256]{1,0:T(8,128)(2,1)}, u32[]{:S(2)}) copy-start(bf16[512,256]{1,0:T(8,128)(2,1)} %cotangent_ref.1) | copy-start | bytes 786436
  33.4 41.8 %copy-start.1 = (bf16[128,256]{1,0:T(8,128)(2,1)S(1)}, bf16[128,256]{1,0:T(8,128)(2,1)}, u32[]{:S(2)}) copy-start(bf16[128,256]{1,0:T(8,128)(2,1)} %weight_ref.1) | copy-start | bytes 196612
  33.5 41.8 %copy-start.2 = (s32[4,12]{1,0:T(4,128)S(1)}, s32[4,12]{1,0:T(4,128)}, u32[]{:S(2)}) copy-start(s32[4,12]{1,0:T(4,128)} %row_ref.1) | copy-start | bytes 580
  33.5 41.8 %copy-start.3 = (f32[256]{0:T(256)S(1)}, f32[256]{0:T(256)}, u32[]{:S(2)}) copy-start(f32[256]{0:T(256)} %param.14) | copy-start | bytes 3076
  33.5 41.8 %copy-start.4 = (s32[4]{0:T(128)S(1)}, s32[4]{0:T(128)}, u32[]{:S(2)}) copy-start(s32[4]{0:T(128)} %count_ref.1) | copy-start | bytes 52

commit v3 on v2

--- a/solution.py
+++ b/solution.py
@@ -7,38 +7,25 @@
 
 AXES = ("zlo", "core", "x", "zhi", "y")
 AXIS_SIZES = (2, 2, 4, 2, 4)
-PLANE = ("x", "y")
-PEERS = 16
+CHIPS = ("zlo", "x", "zhi", "y")
+PEERS = 64
+LANES = 128
 
 
-def z_of(index):
-    return (index % 2) * 2 + index // 2
-
-
-def ring(value, axis, step):
-    if axis == "z":
-        pairs = [(i, z_of((z_of(i) + step) % 4)) for i in range(4)]
-        return lax.ppermute(value, ("zlo", "zhi"), pairs)
-    size = lax.axis_size(axis)
-    return lax.ppermute(value, axis, [(i, (i + step) % size) for i in range(size)])
-
-
-def gather_kernel(need_ref, own_ref, one_ref, two_ref, three_ref, other_ref, out_ref, table_ref, stage_ref, sent):
-    part = own_ref.shape[0]
-    for at, piece in enumerate((own_ref, one_ref, two_ref, three_ref)):
-        table_ref[at * part : (at + 1) * part] = piece[...]
-    table_ref[4 * part :] = other_ref[...]
-    slots = out_ref.shape[1]
-
-    def one_peer(peer, carry):
-        for slot in range(slots):
-            stage_ref[peer, slot] = table_ref[need_ref[peer, slot]]
-        return carry
-
+def pick_kernel(need_ref, own_ref, other_ref, out_ref, stage_ref, sent):
+    table = jnp.concatenate([own_ref[...], other_ref[...]], axis=0)
+    need = need_ref[...]
+    slots, runs = need.shape[0], sent.shape[0]
+    span = PEERS // runs
+    blocks = lax.broadcasted_iota(jnp.int32, (slots, table.shape[0]), 1)
     copies = []
-    for run in range(sent.shape[0]):
-        span = PEERS // sent.shape[0]
-        lax.fori_loop(run * span, (run + 1) * span, one_peer, 0)
+    for run in range(runs):
+        hot = [
+            jnp.where(blocks == need[:, peer : peer + 1], 1.0, 0.0).astype(table.dtype)
+            for peer in range(run * span, (run + 1) * span)
+        ]
+        rows = jnp.dot(jnp.concatenate(hot, axis=0), table, preferred_element_type=jnp.float32)
+        stage_ref[run * span : (run + 1) * span] = rows.astype(table.dtype).reshape(span, slots, table.shape[1])
         peers = pl.ds(run * span, span)
         copies.append(pltpu.make_async_copy(stage_ref.at[peers], out_ref.at[peers], sent.at[run]))
         copies[-1].start()
@@ -46,23 +33,18 @@
         copy.wait()
 
 
-def gather_slices(need, own, one, two, three, other, slots):
-    part, height, width = own.shape
+def pick_slices(need, own, other):
     vmem = pl.BlockSpec(memory_space=pltpu.VMEM)
-    shape = (PEERS, slots, height, width)
+    shape = (PEERS, need.shape[0], own.shape[1])
     return pl.pallas_call(
-        gather_kernel,
+        pick_kernel,
         out_shape=jax.ShapeDtypeStruct(shape, own.dtype),
-        in_specs=[pl.BlockSpec(memory_space=pltpu.SMEM)] + [vmem] * 5,
+        in_specs=[vmem] * 3,
         out_specs=pl.BlockSpec(memory_space=pltpu.HBM),
-        scratch_shapes=[
-            pltpu.VMEM((8 * part, height, width), own.dtype),
-            pltpu.VMEM(shape, own.dtype),
-            pltpu.SemaphoreType.DMA((4,)),
-        ],
-        compiler_params=pltpu.CompilerParams(vmem_limit_bytes=24 * 1024 * 1024),
+        scratch_shapes=[pltpu.VMEM(shape, own.dtype), pltpu.SemaphoreType.DMA((8,))],
+        compiler_params=pltpu.CompilerParams(vmem_limit_bytes=32 * 1024 * 1024),
         name="pick_slices",
-    )(need, own, one, two, three, other)
+    )(need, own, other)
 
 
 def gelu_parts(values):
@@ -76,7 +58,7 @@
 
 
 def layer_kernel(
-    row_ref, count_ref, tiles_ref, slices_ref, weight_ref, bias_ref, cotangent_ref, hidden_ref, grad_ref, held, landed
+    row_ref, count_ref, tiles_ref, slices_ref, weight_ref, bias_ref, cotangent_ref, hidden_ref, grad_ref, held, wide, landed
 ):
     groups, slots = held.shape[:2]
     runs = landed.shape[1]
@@ -90,8 +72,16 @@
             )
             copies[-1].start()
 
+    needed, stride = groups * slots, wide.shape[1] // PEERS
+    turns = wide.shape[0]
+    for peer in range(PEERS):
+        for turn in range(turns):
+            lanes = slices_ref[peer, :, turn * LANES : (turn + 1) * LANES]
+            wide[turn, peer * stride : peer * stride + needed, :] = lanes.astype(jnp.float32)
+
     def spread(group, slot):
-        picked = jnp.concatenate([slices_ref[i, group * slots + slot] for i in range(PEERS)], axis=0)
+        at = pl.ds(group * slots + slot, PEERS, stride=stride)
+        picked = jnp.concatenate([wide[turn, at, :] for turn in range(turns)], axis=0).astype(slices_ref.dtype)
         row = jnp.where(slot < count_ref[group], row_ref[group, slot], 2)
         none = jnp.zeros_like(picked)
         return jnp.concatenate([jnp.where(row == 0, picked, none), jnp.where(row == 1, picked, none)], axis=1)
@@ -138,9 +128,10 @@
         out_specs=(vmem, vmem),
         scratch_shapes=[
             pltpu.VMEM(tiles.shape, tiles.dtype),
+            pltpu.VMEM((slices.shape[2] // LANES, PEERS * (slices.shape[1] + 1), LANES), jnp.float32),
             pltpu.SemaphoreType.DMA((tiles.shape[0], runs)),
         ],
-        compiler_params=pltpu.CompilerParams(vmem_limit_bytes=32 * 1024 * 1024),
+        compiler_params=pltpu.CompilerParams(vmem_limit_bytes=40 * 1024 * 1024),
         name="layer",
     )(rows, counts, tiles, slices, weight, bias.reshape(1, -1), cotangent)
 
@@ -154,30 +145,21 @@
 def local(features, tile_values, tile_row, tile_col, tile_count, weight, bias, cotangent):
     groups, slots, block, _ = tile_values.shape
     width = features.shape[1]
-    height = block // PEERS
+    turns = block // PEERS
     needed = groups * slots
-    core = lax.axis_index("core")
-    depth = lax.axis_index("zhi") * 2 + lax.axis_index("zlo")
 
     team = lax.broadcasted_iota(jnp.int32, (groups, slots), 0)
-    holder, part = tile_col // 2, tile_col % 2
-    there = ((holder // 4) % 2) * 2 + team // 2
-    place = ((holder // 8) * 4 + holder % 4) * 2 + part
-    turn = (team % 2) ^ core
-    need = ((turn * 4 + (there - depth) % 4) * (2 * PEERS) + place).astype(jnp.bfloat16).reshape(1, needed)
-    need = jnp.broadcast_to(jnp.pad(need, ((0, 0), (0, width - needed))), (height, width))
+    need = ((team % 2) ^ lax.axis_index("core")) * (2 * PEERS) + (team // 2) * PEERS + tile_col
+    need = jnp.pad(need.astype(jnp.bfloat16).reshape(needed), (0, width - needed))
 
-    mine = features.reshape(-1, PEERS, height, width).transpose(1, 0, 2, 3)
-    lists = jnp.broadcast_to(need[None, None], (PEERS, 1, height, width))
-    dealt = lax.all_to_all(jnp.concatenate([mine, lists], axis=1), PLANE, 0, 0)
-    own = dealt[:, :2].reshape(2 * PEERS, height, width)
-    wanted = dealt[:, 2, 0, :needed].astype(jnp.int32)
+    mine = features.reshape(-1, turns, PEERS, width).transpose(2, 0, 1, 3).reshape(PEERS, -1, turns * width)
+    lists = jnp.broadcast_to(need, (PEERS, mine.shape[1], width))
+    dealt = lax.all_to_all(jnp.concatenate([mine, lists], axis=2), CHIPS, 0, 0)
+    own = dealt[:, :, : turns * width].reshape(-1, turns * width)
+    wanted = dealt[:, 0, turns * width : turns * width + needed].astype(jnp.int32).T
+    other = lax.ppermute(own, "core", [(0, 1), (1, 0)])
 
-    one, two, three = (ring(own, "z", -step) for step in (1, 2, 3))
-    other = ring(jnp.concatenate([own, one, two, three], axis=0), "core", 1)
-
-    picked = gather_slices(wanted, own, one, two, three, other, needed)
-    slices = lax.all_to_all(picked, PLANE, 0, 0)
+    slices = lax.all_to_all(pick_slices(wanted, own, other), CHIPS, 0, 0)
 
     hidden, grad = layer(tile_row, tile_count, tile_values, slices, weight, bias, cotangent)
     summed = sum_over_devices(grad)

time: 116 us -> 118 us (1.017)
  blocking collectives: 89.7 us -> 99.1 us
  starting transfers between devices: 8.29 us -> 2.18 us
  waiting for transfers between devices: 5.81 us -> 0.98 us
  Pallas kernels: 7.86 us -> 10.4 us
  local copies, waits for them, and re-layouts: 1.78 us -> 3.05 us
    all_to_all x2, blocking collectives: 56.5 us -> 64.5 us  [the longest x1 43.8 us: local(): slices = lax.all_to_all(pick_slices(wanted, own, other), CHIPS, 0, 0)]
    ppermute x4 -> x1, starting transfers between devices: 8.29 us -> 2.18 us  [local(): other = lax.ppermute(own, 'core', [(0, 1), (1, 0)])]
    ppermute x4 -> x1, waiting for transfers between devices: 5.81 us -> 0.98 us  [local(): other = lax.ppermute(own, 'core', [(0, 1), (1, 0)])]
    pallas_call x1, Pallas kernels: 1.89 us -> 4 us  [pick_slices(): pl.pallas_call(pick_kernel, out_shape=jax.ShapeDtypeStruct(shape, own.dty...]
    all_to_all x1, blocking collectives: 18 us -> 19.4 us  [sum_over_devices(): total = jnp.sum(lax.all_to_all(rows, AXES, 0, 0), axis=0)]
  transfers between devices with their start and end apart: 4 -> 1, of which waited for: 4 -> 1; matrix products, arithmetic and copies ran while one was open for 0% -> 0% of each run, Pallas kernels for 0% -> 0%
where the time goes in v3:
time: 118 us
  blocking collectives  99.1 us (84%)
  Pallas kernels  10.4 us (9%)
  local copies, waits for them, and re-layouts  3.05 us (3%)
  starting transfers between devices  2.18 us (2%)
    all_to_all x1, blocking collectives, local(): slices = lax.all_to_all(pick_slices(wanted, own, other), CHIPS, 0, 0)  43.8 us
    all_to_all x1, blocking collectives, local(): dealt = lax.all_to_all(jnp.concatenate([mine, lists], axis=2), CHIPS, 0, 0)  20.6 us
    all_to_all x1, blocking collectives, sum_over_devices(): total = jnp.sum(lax.all_to_all(rows, AXES, 0, 0), axis=0)  19.4 us
    all_to_all x1, blocking collectives, sum_over_devices(): return lax.all_to_all(jnp.broadcast_to(total[None], rows.shape), AXES, 0, 0)  15.3 us
    pallas_call x1, Pallas kernels, layer(): pl.pallas_call(layer_kernel, out_shape=(jax.ShapeDtypeStruct((nodes, out_...  6.4 us
    pallas_call x1, Pallas kernels, pick_slices(): pl.pallas_call(pick_kernel, out_shape=jax.ShapeDtypeStruct(shape, own.dty...  4 us
  transfers between devices with their start and end apart: 1, of which 1 were waited for; matrix products, arithmetic and copies ran while one was open for 0% of the time, Pallas kernels for 0%

profile of v3, /device:TPU:1, one launch (start us, length us, event | category | flops | bytes accessed | tf_op | source)
XLA Modules:
  0.0 117.6 jit_solution(15596780515233020672)
XLA Ops:
  0.7 0.8 add_convert_fusion
  1.4 0.1 reshape.32
  1.5 1.0 copy.25
  2.5 0.1 reshape.31
  2.6 0.2 pad_maximum_fusion
  2.8 20.6 %all_to_all.20 = bf16[64,2,640]{2,1,0:T(2,128)(2,1)S(1)} all-to-all(bf16[64,2,640]{2,1,0:T(2,128)(2,1)S(1)} %pad_maximum_fusion), channel_id=1, replica_groups=mesh['zlo'=2,'core'=2,'x'=4,'zhi'=2,'y'=4] {'zlo','x','zhi','y'}, dimensions={0} | all-to-all | bytes 327680 | tf_op jit(solution)/shard_map/all_to_all | solution.py:157
  23.5 0.1 copy.20
  23.5 0.1 slice.17
  23.6 0.1 reshape.33.own_ref
  23.7 2.2 %collective-permute-start = (bf16[128,512]{1,0:T(8,128)(2,1)S(1)}, bf16[128,512]{1,0:T(8,128)(2,1)S(1)}, u32[]{:S(2)}, u32[]{:S(2)}) collective-permute-start(bf16[128,512]{1,0:T(8,128)(2,1)S(1)} %reshape.33.own_ref), channel_id=1, source_target_pairs={{0,32},{32,0},{1,33},{33,1},{2,34},{34,2},{3,35},{35,3},{4,36},{36... | collective-permute-start | bytes 393224 | tf_op jit(solution)/shard_map/ppermute | solution.py:160
  25.9 1.0 collective-permute-done.other_ref
  26.9 0.0 copy-start.1
  26.9 0.0 copy-start.2
  26.9 0.0 copy-start.3
  26.9 4.0 %pick_slices.1 = bf16[64,48,512]{2,1,0:T(8,128)(2,1)S(1)} custom-call(s32[48,64]{1,0:T(8,128)S(1)} %convert_bitcast_fusion.need_ref, bf16[128,512]{1,0:T(8,128)(2,1)S(1)} %reshape.33.own_ref, bf16[128,512]{1,0:T(8,128)(2,1)S(1)} %collective-permute-done.other_ref), custom_call_target="tpu_custom_call" | custom-call | tf_op jit(solution)/shard_map/pick_slices/pallas_call | solution.py:39
  30.9 0.0 copy-start
  30.9 0.0 copy-start.4
  30.9 0.0 copy-start.5
  30.9 43.8 %all_to_all.21.slices_ref = bf16[64,48,512]{2,1,0:T(8,128)(2,1)S(1)} all-to-all(bf16[64,48,512]{2,1,0:T(8,128)(2,1)S(1)} %pick_slices.1), channel_id=1, replica_groups=mesh['zlo'=2,'core'=2,'x'=4,'zhi'=2,'y'=4] {'zlo','x','zhi','y'}, dimensions={0} | all-to-all | bytes 6291456 | tf_op jit(solution)/shard_map/all_to_all | solution.py:162
  74.8 0.0 copy-done.1
  74.8 0.0 copy-done.2
  74.8 0.0 copy-done.3
  74.8 0.0 copy-done
  74.8 0.0 copy-done.4
  74.8 0.0 copy-done.5
  74.8 6.4 %layer.1 = (bf16[512,256]{1,0:T(8,128)(2,1)}, f32[128,384]{1,0:T(8,128)S(1)}) custom-call(s32[4,12]{1,0:T(4,128)S(1)} %copy-done.3, s32[4]{0:T(128)S(1)} %copy-done.5, bf16[4,12,256,256]{3,2,1,0:T(8,128)(2,1)S(1)} %copy-done, bf16[64,48,512]{2,1,0:T(8,128)(2,1)S(1)} %all_to_all.21.slices_ref, bf16[128,256]{1,0:T(8,128)(2,1)S(1)} %copy-done.2, ...), custom_call_target="tpu_custom_call" | custom-call | tf_op jit(solution)/shard_map/layer/pallas_call | solution.py:121
  81.2 0.1 copy.18
  81.3 0.2 copy.19
  81.5 19.4 %all_to_all.22 = f32[128,3,128]{2,1,0:T(4,128)S(1)} all-to-all(f32[128,3,128]{2,1,0:T(4,128)S(1)} %copy.19), channel_id=1, replica_groups=mesh['zlo'=2,'core'=2,'x'=4,'zhi'=2,'y'=4] {'zlo','core','x','zhi','y'}, dimensions={0} | all-to-all | bytes 393216 | tf_op jit(solution)/shard_map/all_to_all | solution.py:141
  100.9 0.1 reduce_sum.9
  101.1 15.3 %all_to_all.23 = f32[128,3,128]{2,1,0:T(4,128)S(1)} all-to-all(f32[128,3,128]{2,1,0:T(4,128)S(1)} %broadcast_in_dim.10), channel_id=1, replica_groups=mesh['zlo'=2,'core'=2,'x'=4,'zhi'=2,'y'=4] {'zlo','core','x','zhi','y'}, dimensions={0} | all-to-all | bytes 393216 | tf_op jit(solution)/shard_map/all_to_all | solution.py:142
  116.4 0.7 copy.24
  117.1 0.6 slice.19
  (8 shorter events, 0.1 us)
Async XLA Ops:
  23.7 3.2 %collective-permute-start = (bf16[128,512]{1,0:T(8,128)(2,1)S(1)}, bf16[128,512]{1,0:T(8,128)(2,1)S(1)}, u32[]{:S(2)}, u32[]{:S(2)}) collective-permute-start(bf16[128,512]{1,0:T(8,128)(2,1)S(1)} %reshape.33.own_ref), channel_id=1, source_target_pairs={{0,32},{32,0},{1,33},{33,1},{2,34},{34,2},{3,35},{35,3},{4,36},{36... | collective-permute-start | bytes 393224 | tf_op jit(solution)/shard_map/ppermute | solution.py:160
  26.9 47.9 %copy-start.1 = (bf16[512,256]{1,0:T(8,128)(2,1)S(1)}, bf16[512,256]{1,0:T(8,128)(2,1)}, u32[]{:S(2)}) copy-start(bf16[512,256]{1,0:T(8,128)(2,1)} %cotangent_ref.1) | copy-start | bytes 786436
  26.9 47.9 %copy-start.2 = (bf16[128,256]{1,0:T(8,128)(2,1)S(1)}, bf16[128,256]{1,0:T(8,128)(2,1)}, u32[]{:S(2)}) copy-start(bf16[128,256]{1,0:T(8,128)(2,1)} %weight_ref.1) | copy-start | bytes 196612
  26.9 47.9 %copy-start.3 = (s32[4,12]{1,0:T(4,128)S(1)}, s32[4,12]{1,0:T(4,128)}, u32[]{:S(2)}) copy-start(s32[4,12]{1,0:T(4,128)} %row_ref.1) | copy-start | bytes 580
  30.9 43.9 %copy-start = (bf16[4,12,256,256]{3,2,1,0:T(8,128)(2,1)S(1)}, bf16[4,12,256,256]{3,2,1,0:T(8,128)(2,1)}, u32[]{:S(2)}) copy-start(bf16[4,12,256,256]{3,2,1,0:T(8,128)(2,1)} %tiles_ref.1) | copy-start | bytes 18874372
  30.9 43.9 %copy-start.4 = (f32[256]{0:T(256)S(1)}, f32[256]{0:T(256)}, u32[]{:S(2)}) copy-start(f32[256]{0:T(256)} %param.14) | copy-start | bytes 3076
  30.9 43.9 %copy-start.5 = (s32[4]{0:T(128)S(1)}, s32[4]{0:T(128)}, u32[]{:S(2)}) copy-start(s32[4]{0:T(128)} %count_ref.1) | copy-start | bytes 52

commit v4 on v3

--- a/solution.py
+++ b/solution.py
@@ -1,3 +1,5 @@
+import math
+
 import jax
 import jax.numpy as jnp
 from jax import lax
@@ -8,29 +10,27 @@
 AXES = ("zlo", "core", "x", "zhi", "y")
 AXIS_SIZES = (2, 2, 4, 2, 4)
 CHIPS = ("zlo", "x", "zhi", "y")
-PEERS = 64
+SIZE = dict(zip(AXES, AXIS_SIZES))
+ALIKE = ("zhi",)
+DEAL = tuple(axis for axis in CHIPS if axis not in ALIKE)
+PEERS = math.prod(SIZE[axis] for axis in DEAL)
+SPAN = 8
+RUN = 6
 LANES = 128
 
 
-def pick_kernel(need_ref, own_ref, other_ref, out_ref, stage_ref, sent):
+def pick_kernel(need_ref, own_ref, other_ref, out_ref):
     table = jnp.concatenate([own_ref[...], other_ref[...]], axis=0)
     need = need_ref[...]
-    slots, runs = need.shape[0], sent.shape[0]
-    span = PEERS // runs
+    slots, span = need.shape[0], SPAN
     blocks = lax.broadcasted_iota(jnp.int32, (slots, table.shape[0]), 1)
-    copies = []
-    for run in range(runs):
+    for run in range(PEERS // span):
         hot = [
             jnp.where(blocks == need[:, peer : peer + 1], 1.0, 0.0).astype(table.dtype)
             for peer in range(run * span, (run + 1) * span)
         ]
         rows = jnp.dot(jnp.concatenate(hot, axis=0), table, preferred_element_type=jnp.float32)
-        stage_ref[run * span : (run + 1) * span] = rows.astype(table.dtype).reshape(span, slots, table.shape[1])
-        peers = pl.ds(run * span, span)
-        copies.append(pltpu.make_async_copy(stage_ref.at[peers], out_ref.at[peers], sent.at[run]))
-        copies[-1].start()
-    for copy in copies:
-        copy.wait()
+        out_ref[run * span : (run + 1) * span] = rows.astype(table.dtype).reshape(span, slots, table.shape[1])
 
 
 def pick_slices(need, own, other):
@@ -40,8 +40,7 @@
         pick_kernel,
         out_shape=jax.ShapeDtypeStruct(shape, own.dtype),
         in_specs=[vmem] * 3,
-        out_specs=pl.BlockSpec(memory_space=pltpu.HBM),
-        scratch_shapes=[pltpu.VMEM(shape, own.dtype), pltpu.SemaphoreType.DMA((8,))],
+        out_specs=vmem,
         compiler_params=pltpu.CompilerParams(vmem_limit_bytes=32 * 1024 * 1024),
         name="pick_slices",
     )(need, own, other)
@@ -58,19 +57,9 @@
 
 
 def layer_kernel(
-    row_ref, count_ref, tiles_ref, slices_ref, weight_ref, bias_ref, cotangent_ref, hidden_ref, grad_ref, held, wide, landed
+    row_ref, count_ref, tiles_ref, slices_ref, weight_ref, bias_ref, cotangent_ref, hidden_ref, grad_ref, wide
 ):
-    groups, slots = held.shape[:2]
-    runs = landed.shape[1]
-    span = slots // runs
-    copies = []
-    for group in range(groups):
-        for run in range(runs):
-            part = pl.ds(run * span, span)
-            copies.append(
-                pltpu.make_async_copy(tiles_ref.at[group, part], held.at[group, part], landed.at[group, run])
-            )
-            copies[-1].start()
+    groups, slots = tiles_ref.shape[:2]
 
     needed, stride = groups * slots, wide.shape[1] // PEERS
     turns = wide.shape[0]
@@ -88,11 +77,10 @@
 
     total = None
     for group in range(groups):
-        for run in range(runs):
-            copies[group * runs + run].wait()
-            part = range(run * span, (run + 1) * span)
-            tiles = jnp.concatenate([held[group, slot] for slot in part], axis=1)
-            picked = jnp.concatenate([spread(group, slot) for slot in part], axis=0)
+        for first in range(0, slots, RUN):
+            run = range(first, first + RUN)
+            tiles = jnp.concatenate([tiles_ref[group, slot] for slot in run], axis=1)
+            picked = jnp.concatenate([spread(group, slot) for slot in run], axis=0)
             product = jnp.dot(tiles, picked, preferred_element_type=jnp.float32)
             total = product if total is None else total + product
 
@@ -115,7 +103,6 @@
 def layer(rows, counts, tiles, slices, weight, bias, cotangent):
     nodes, out_width = cotangent.shape
     width = weight.shape[0]
-    runs = 2
     vmem = pl.BlockSpec(memory_space=pltpu.VMEM)
     smem = pl.BlockSpec(memory_space=pltpu.SMEM)
     return pl.pallas_call(
@@ -124,14 +111,12 @@
             jax.ShapeDtypeStruct((nodes, out_width), jnp.bfloat16),
             jax.ShapeDtypeStruct((width, out_width + width), jnp.float32),
         ),
-        in_specs=[smem, smem, pl.BlockSpec(memory_space=pltpu.HBM), vmem, vmem, vmem, vmem],
+        in_specs=[smem, smem, vmem, vmem, vmem, vmem, vmem],
         out_specs=(vmem, vmem),
         scratch_shapes=[
-            pltpu.VMEM(tiles.shape, tiles.dtype),
             pltpu.VMEM((slices.shape[2] // LANES, PEERS * (slices.shape[1] + 1), LANES), jnp.float32),
-            pltpu.SemaphoreType.DMA((tiles.shape[0], runs)),
         ],
-        compiler_params=pltpu.CompilerParams(vmem_limit_bytes=40 * 1024 * 1024),
+        compiler_params=pltpu.CompilerParams(vmem_limit_bytes=32 * 1024 * 1024),
         name="layer",
     )(rows, counts, tiles, slices, weight, bias.reshape(1, -1), cotangent)
 
@@ -148,18 +133,25 @@
     turns = block // PEERS
     needed = groups * slots
 
+    chips = math.prod(SIZE[axis] for axis in CHIPS)
     team = lax.broadcasted_iota(jnp.int32, (groups, slots), 0)
-    need = ((team % 2) ^ lax.axis_index("core")) * (2 * PEERS) + (team // 2) * PEERS + tile_col
+    need = ((team % 2) ^ lax.axis_index("core")) * (2 * chips) + (team // 2) * chips + tile_col
     need = jnp.pad(need.astype(jnp.bfloat16).reshape(needed), (0, width - needed))
 
     mine = features.reshape(-1, turns, PEERS, width).transpose(2, 0, 1, 3).reshape(PEERS, -1, turns * width)
-    lists = jnp.broadcast_to(need, (PEERS, mine.shape[1], width))
-    dealt = lax.all_to_all(jnp.concatenate([mine, lists], axis=2), CHIPS, 0, 0)
+    mine = jnp.concatenate([mine, jnp.broadcast_to(need, (PEERS, mine.shape[1], width))], axis=2)
+    grid = [SIZE[axis] for axis in CHIPS]
+    once = [1 if axis in ALIKE else SIZE[axis] for axis in CHIPS]
+    mine = jnp.broadcast_to(mine.reshape(once + list(mine.shape[1:])), grid + list(mine.shape[1:]))
+    dealt = lax.all_to_all(mine.reshape((chips,) + mine.shape[len(grid) :]), CHIPS, 0, 0)
     own = dealt[:, :, : turns * width].reshape(-1, turns * width)
-    wanted = dealt[:, 0, turns * width : turns * width + needed].astype(jnp.int32).T
+    lists = dealt[:, 0, turns * width : turns * width + needed].reshape(grid + [needed])
+    for axis in ALIKE:
+        lists = lax.dynamic_slice_in_dim(lists, lax.axis_index(axis), 1, CHIPS.index(axis))
+    wanted = lists.reshape(PEERS, needed).astype(jnp.int32).T
     other = lax.ppermute(own, "core", [(0, 1), (1, 0)])
 
-    slices = lax.all_to_all(pick_slices(wanted, own, other), CHIPS, 0, 0)
+    slices = lax.all_to_all(pick_slices(wanted, own, other), DEAL, 0, 0)
 
     hidden, grad = layer(tile_row, tile_count, tile_values, slices, weight, bias, cotangent)
     summed = sum_over_devices(grad)

time: 118 us -> 110 us (0.932)
  Pallas kernels: 10.4 us -> 5.02 us
  blocking collectives: 99.1 us -> 96.5 us
    pallas_call x1, Pallas kernels: 4 us -> 1.03 us  [pick_slices(): pl.pallas_call(pick_kernel, out_shape=jax.ShapeDtypeStruct(shape, own.dty...]
    pallas_call x1, Pallas kernels: 6.4 us -> 4 us  [layer(): pl.pallas_call(layer_kernel, out_shape=(jax.ShapeDtypeStruct((nodes, out_...]
    all_to_all x2, blocking collectives: 64.5 us -> 62.9 us  [the longest x1 41.5 us: local(): slices = lax.all_to_all(pick_slices(wanted, own, other), DEAL, 0, 0)]
where the time goes in v4:
time: 110 us
  blocking collectives  96.5 us (88%)
  Pallas kernels  5.02 us (5%)
  local copies, waits for them, and re-layouts  3.27 us (3%)
  starting transfers between devices  2.29 us (2%)
    all_to_all x1, blocking collectives, local(): slices = lax.all_to_all(pick_slices(wanted, own, other), DEAL, 0, 0)  41.5 us
    all_to_all x1, blocking collectives, local(): lax.all_to_all(mine.reshape((chips,) + mine.shape[len(grid):]), CHIPS, 0, 0)  21.4 us
    all_to_all x1, blocking collectives, sum_over_devices(): total = jnp.sum(lax.all_to_all(rows, AXES, 0, 0), axis=0)  18.3 us
    all_to_all x1, blocking collectives, sum_over_devices(): return lax.all_to_all(jnp.broadcast_to(total[None], rows.shape), AXES, 0, 0)  15.3 us
    pallas_call x1, Pallas kernels, layer(): pl.pallas_call(layer_kernel, out_shape=(jax.ShapeDtypeStruct((nodes, out_...  4 us
    ppermute x1, starting transfers between devices, local(): other = lax.ppermute(own, 'core', [(0, 1), (1, 0)])  2.29 us
  transfers between devices with their start and end apart: 1, of which 1 were waited for; matrix products, arithmetic and copies ran while one was open for 0% of the time, Pallas kernels for 0%

profile of v4, /device:TPU:1, one launch (start us, length us, event | category | flops | bytes accessed | tf_op | source)
XLA Modules:
  0.0 110.0 jit_solution(18279419363802252413)
XLA Ops:
  0.7 0.8 add_convert_fusion
  1.4 0.1 reshape.37
  1.5 1.0 copy.27
  2.5 0.0 slice-start
  2.5 0.1 maximum_bitcast_fusion
  2.7 0.2 broadcast_in_dim.18
  2.9 21.4 %all_to_all.20 = bf16[64,2,1152]{2,1,0:T(2,128)(2,1)S(1)} all-to-all(bf16[64,2,1152]{2,1,0:T(2,128)(2,1)S(1)} %bitcast.24), channel_id=1, replica_groups=mesh['zlo'=2,'core'=2,'x'=4,'zhi'=2,'y'=4] {'zlo','x','zhi','y'}, dimensions={0} | all-to-all | bytes 589824 | tf_op jit(solution)/shard_map/all_to_all | solution.py:146
  24.3 0.2 slice.17
  24.5 0.1 reshape.39.own_ref
  24.6 2.3 %collective-permute-start = (bf16[128,1024]{1,0:T(8,128)(2,1)S(1)}, bf16[128,1024]{1,0:T(8,128)(2,1)S(1)}, u32[]{:S(2)}, u32[]{:S(2)}) collective-permute-start(bf16[128,1024]{1,0:T(8,128)(2,1)S(1)} %reshape.39.own_ref), channel_id=1, source_target_pairs={{0,32},{32,0},{1,33},{33,1},{2,34},{34,2},{3,35},{35,3},{4,36},{36... | collective-permute-start | bytes 786440 | tf_op jit(solution)/shard_map/ppermute | solution.py:152
  27.0 0.1 copy.19
  27.0 1.0 collective-permute-done.other_ref
  28.0 0.0 slice-start.1
  28.0 1.0 pick_slices.1
  29.1 0.0 copy-start
  29.1 0.0 copy-start.1
  29.1 0.0 copy-start.2
  29.1 0.0 copy-start.3
  29.1 0.0 copy-start.4
  29.1 41.5 %all_to_all.21.slices_ref = bf16[32,48,1024]{2,1,0:T(8,128)(2,1)S(1)} all-to-all(bf16[32,48,1024]{2,1,0:T(8,128)(2,1)S(1)} %pick_slices.1), channel_id=1, replica_groups=mesh['zlo'=2,'core'=2,'x'=4,'zhi'=2,'y'=4] {'zlo','x','y'}, dimensions={0} | all-to-all | bytes 6291456 | tf_op jit(solution)/shard_map/all_to_all | solution.py:154
  70.6 0.0 slice-done
  70.6 0.0 slice-done.1
  70.6 0.0 copy-done
  70.7 0.0 copy-done.1
  70.7 0.0 copy-done.2
  70.7 0.0 copy-done.3
  70.7 0.0 copy-done.4
  70.7 4.0 %layer.1 = (bf16[512,256]{1,0:T(8,128)(2,1)}, f32[128,384]{1,0:T(8,128)S(1)}) custom-call(s32[4,12]{1,0:T(4,128)S(1)} %copy-done.2, s32[4]{0:T(128)S(1)} %copy-done.4, bf16[4,12,256,256]{3,2,1,0:T(8,128)(2,1)S(1)} %bitcast.21, bf16[32,48,1024]{2,1,0:T(8,128)(2,1)S(1)} %all_to_all.21.slices_ref, bf16[128,256]{1,0:T(8,128)(2,1)S(1)} %copy-done.1, ...), custom_call_target="tpu_custom_call" | custom-call | tf_op jit(solution)/shard_map/layer/pallas_call | solution.py:108
  74.7 0.1 copy.20
  74.8 0.2 copy.21
  75.0 18.3 %all_to_all.22 = f32[128,3,128]{2,1,0:T(4,128)S(1)} all-to-all(f32[128,3,128]{2,1,0:T(4,128)S(1)} %copy.21), channel_id=1, replica_groups=mesh['zlo'=2,'core'=2,'x'=4,'zhi'=2,'y'=4] {'zlo','core','x','zhi','y'}, dimensions={0} | all-to-all | bytes 393216 | tf_op jit(solution)/shard_map/all_to_all | solution.py:126
  93.3 0.1 reduce_sum.9
  93.5 15.3 %all_to_all.23 = f32[128,3,128]{2,1,0:T(4,128)S(1)} all-to-all(f32[128,3,128]{2,1,0:T(4,128)S(1)} %broadcast_in_dim.19), channel_id=1, replica_groups=mesh['zlo'=2,'core'=2,'x'=4,'zhi'=2,'y'=4] {'zlo','core','x','zhi','y'}, dimensions={0} | all-to-all | bytes 393216 | tf_op jit(solution)/shard_map/all_to_all | solution.py:127
  108.8 0.7 copy.26
  109.4 0.6 slice.19
  (12 shorter events, 0.2 us)
Async XLA Ops:
  2.5 68.1 %slice-start = ((s8[6291456]{0:T(1024)(128)(4,1)}), s8[2097152]{0:T(1024)(128)(4,1)S(1)}, s32[]{:S(2)}) async-start(s8[6291456]{0:T(1024)(128)(4,1)} %bitcast.20), calls=%async_computation.4 | async-start | bytes 4194304
  24.6 3.5 %collective-permute-start = (bf16[128,1024]{1,0:T(8,128)(2,1)S(1)}, bf16[128,1024]{1,0:T(8,128)(2,1)S(1)}, u32[]{:S(2)}, u32[]{:S(2)}) collective-permute-start(bf16[128,1024]{1,0:T(8,128)(2,1)S(1)} %reshape.39.own_ref), channel_id=1, source_target_pairs={{0,32},{32,0},{1,33},{33,1},{2,34},{34,2},{3,35},{35,3},{4,36},{36... | collective-permute-start | bytes 786440 | tf_op jit(solution)/shard_map/ppermute | solution.py:152
  28.0 42.6 %slice-start.1 = ((s8[6291456]{0:T(1024)(128)(4,1)}), s8[4194304]{0:T(1024)(128)(4,1)S(1)}, s32[]{:S(2)}) async-start(s8[6291456]{0:T(1024)(128)(4,1)} %bitcast.20), calls=%async_computation.5 | async-start | bytes 8388608
  29.1 41.6 %copy-start = (bf16[512,256]{1,0:T(8,128)(2,1)S(1)}, bf16[512,256]{1,0:T(8,128)(2,1)}, u32[]{:S(2)}) copy-start(bf16[512,256]{1,0:T(8,128)(2,1)} %cotangent_ref.1) | copy-start | bytes 786436
  29.1 41.6 %copy-start.1 = (bf16[128,256]{1,0:T(8,128)(2,1)S(1)}, bf16[128,256]{1,0:T(8,128)(2,1)}, u32[]{:S(2)}) copy-start(bf16[128,256]{1,0:T(8,128)(2,1)} %weight_ref.1) | copy-start | bytes 196612
  29.1 41.6 %copy-start.2 = (s32[4,12]{1,0:T(4,128)S(1)}, s32[4,12]{1,0:T(4,128)}, u32[]{:S(2)}) copy-start(s32[4,12]{1,0:T(4,128)} %row_ref.1) | copy-start | bytes 580
  29.1 41.6 %copy-start.3 = (f32[256]{0:T(256)S(1)}, f32[256]{0:T(256)}, u32[]{:S(2)}) copy-start(f32[256]{0:T(256)} %param.14) | copy-start | bytes 3076
  29.1 41.6 %copy-start.4 = (s32[4]{0:T(128)S(1)}, s32[4]{0:T(128)}, u32[]{:S(2)}) copy-start(s32[4]{0:T(128)} %count_ref.1) | copy-start | bytes 52

commit v5 on v4

--- a/solution.py
+++ b/solution.py
@@ -9,18 +9,17 @@
 
 AXES = ("zlo", "core", "x", "zhi", "y")
 AXIS_SIZES = (2, 2, 4, 2, 4)
-CHIPS = ("zlo", "x", "zhi", "y")
 SIZE = dict(zip(AXES, AXIS_SIZES))
 ALIKE = ("zhi",)
-DEAL = tuple(axis for axis in CHIPS if axis not in ALIKE)
+DEAL = tuple(axis for axis in AXES if axis not in ALIKE)
 PEERS = math.prod(SIZE[axis] for axis in DEAL)
 SPAN = 8
 RUN = 6
 LANES = 128
 
 
-def pick_kernel(need_ref, own_ref, other_ref, out_ref):
-    table = jnp.concatenate([own_ref[...], other_ref[...]], axis=0)
+def pick_kernel(need_ref, table_ref, out_ref):
+    table = table_ref[...]
     need = need_ref[...]
     slots, span = need.shape[0], SPAN
     blocks = lax.broadcasted_iota(jnp.int32, (slots, table.shape[0]), 1)
@@ -33,17 +32,17 @@
         out_ref[run * span : (run + 1) * span] = rows.astype(table.dtype).reshape(span, slots, table.shape[1])
 
 
-def pick_slices(need, own, other):
+def pick_slices(need, table):
     vmem = pl.BlockSpec(memory_space=pltpu.VMEM)
-    shape = (PEERS, need.shape[0], own.shape[1])
+    shape = (PEERS, need.shape[0], table.shape[1])
     return pl.pallas_call(
         pick_kernel,
-        out_shape=jax.ShapeDtypeStruct(shape, own.dtype),
-        in_specs=[vmem] * 3,
+        out_shape=jax.ShapeDtypeStruct(shape, table.dtype),
+        in_specs=[vmem] * 2,
         out_specs=vmem,
         compiler_params=pltpu.CompilerParams(vmem_limit_bytes=32 * 1024 * 1024),
         name="pick_slices",
-    )(need, own, other)
+    )(need, table)
 
 
 def gelu_parts(values):
@@ -122,9 +121,12 @@
 
 
 def sum_over_devices(grad):
-    rows = grad.reshape(grad.shape[0], -1, 128)
-    total = jnp.sum(lax.all_to_all(rows, AXES, 0, 0), axis=0)
-    return lax.all_to_all(jnp.broadcast_to(total[None], rows.shape), AXES, 0, 0)
+    group = ('zlo', 'core', 'x', 'zhi', 'y')
+    size = math.prod(SIZE[axis] for axis in group)
+    rows = grad.reshape(size, -1, grad.shape[1])
+    total = jnp.sum(lax.all_to_all(rows, group, 0, 0), axis=0)
+    shared = lax.all_to_all(jnp.broadcast_to(total[None], rows.shape), group, 0, 0)
+    return shared.reshape(grad.shape)
 
 
 def local(features, tile_values, tile_row, tile_col, tile_count, weight, bias, cotangent):
@@ -133,29 +135,33 @@
     turns = block // PEERS
     needed = groups * slots
 
-    chips = math.prod(SIZE[axis] for axis in CHIPS)
     team = lax.broadcasted_iota(jnp.int32, (groups, slots), 0)
-    need = ((team % 2) ^ lax.axis_index("core")) * (2 * chips) + (team // 2) * chips + tile_col
+    need = team * (2 * lax.axis_size(AXES) // groups) + tile_col
     need = jnp.pad(need.astype(jnp.bfloat16).reshape(needed), (0, width - needed))
 
     mine = features.reshape(-1, turns, PEERS, width).transpose(2, 0, 1, 3).reshape(PEERS, -1, turns * width)
-    mine = jnp.concatenate([mine, jnp.broadcast_to(need, (PEERS, mine.shape[1], width))], axis=2)
-    grid = [SIZE[axis] for axis in CHIPS]
-    once = [1 if axis in ALIKE else SIZE[axis] for axis in CHIPS]
-    mine = jnp.broadcast_to(mine.reshape(once + list(mine.shape[1:])), grid + list(mine.shape[1:]))
-    dealt = lax.all_to_all(mine.reshape((chips,) + mine.shape[len(grid) :]), CHIPS, 0, 0)
-    own = dealt[:, :, : turns * width].reshape(-1, turns * width)
+    grid = [SIZE[axis] for axis in AXES]
+    once = [1 if axis in ALIKE else SIZE[axis] for axis in AXES]
+    copies = [SIZE[axis] if axis in ALIKE else 1 for axis in AXES]
+    near = jnp.ones(copies + [1, 1], need.dtype)
+    for axis in ALIKE:
+        at = lax.broadcasted_iota(jnp.int32, near.shape, AXES.index(axis))
+        near = jnp.where(at == lax.axis_index(axis), near, 0)
+    rows = jnp.broadcast_to(mine.reshape(once + list(mine.shape[1:])), grid + list(mine.shape[1:]))
+    lists = jnp.broadcast_to(need * near, grid + [mine.shape[1], width])
+    sent = jnp.concatenate([rows, lists], axis=len(grid) + 1)
+    dealt = lax.all_to_all(sent.reshape((-1,) + sent.shape[len(grid) :]), AXES, 0, 0)
+    table = dealt[:, :, : turns * width].reshape(-1, turns * width)
     lists = dealt[:, 0, turns * width : turns * width + needed].reshape(grid + [needed])
     for axis in ALIKE:
-        lists = lax.dynamic_slice_in_dim(lists, lax.axis_index(axis), 1, CHIPS.index(axis))
+        lists = jnp.max(lists, axis=AXES.index(axis), keepdims=True)
     wanted = lists.reshape(PEERS, needed).astype(jnp.int32).T
-    other = lax.ppermute(own, "core", [(0, 1), (1, 0)])
 
-    slices = lax.all_to_all(pick_slices(wanted, own, other), DEAL, 0, 0)
+    slices = lax.all_to_all(pick_slices(wanted, table), DEAL, 0, 0)
 
     hidden, grad = layer(tile_row, tile_count, tile_values, slices, weight, bias, cotangent)
     summed = sum_over_devices(grad)
-    return (hidden, summed[:, :2].reshape(weight.shape), summed[:2, 2].reshape(bias.shape))
+    return (hidden, summed[:, : bias.shape[0]], summed[:2, bias.shape[0] :].reshape(bias.shape))
 
 
 def solution(mesh):

time: 110 us -> 108 us (0.982)
  starting transfers between devices: 2.29 us -> 0 us
    ppermute x1 -> x0, starting transfers between devices: 2.29 us -> none  [local(): other = lax.ppermute(own, 'core', [(0, 1), (1, 0)])]
  transfers between devices with their start and end apart: 1 -> 0, of which waited for: 1 -> 0; matrix products, arithmetic and copies ran while one was open for 0% -> 0% of each run, Pallas kernels for 0% -> 0%
where the time goes in v5:
time: 108 us
  blocking collectives  97 us (90%)
  Pallas kernels  5.09 us (5%)
  local copies, waits for them, and re-layouts  3.36 us (3%)
  other arithmetic  1.37 us (1%)
    all_to_all x1, blocking collectives, local(): slices = lax.all_to_all(pick_slices(wanted, table), DEAL, 0, 0)  44.5 us
    all_to_all x1, blocking collectives, local(): lax.all_to_all(sent.reshape((-1,) + sent.shape[len(grid):]), AXES, 0, 0)  23 us
    all_to_all x1, blocking collectives, sum_over_devices(): total = jnp.sum(lax.all_to_all(rows, group, 0, 0), axis=0)  14.8 us
    all_to_all x1, blocking collectives, sum_over_devices(): lax.all_to_all(jnp.broadcast_to(total[None], rows.shape), group, 0, 0)  14.6 us
    pallas_call x1, Pallas kernels, layer(): pl.pallas_call(layer_kernel, out_shape=(jax.ShapeDtypeStruct((nodes, out_...  4.05 us

profile of v5, /device:TPU:1, one launch (start us, length us, event | category | flops | bytes accessed | tf_op | source)
XLA Modules:
  0.0 107.6 jit_solution(9126557278445534182)
XLA Ops:
  0.7 0.8 add_convert_fusion
  1.4 0.1 reshape.78
  1.5 1.0 copy.24
  2.5 0.1 broadcast_in_dim.12
  2.6 0.1 broadcast_multiply_fusion
  2.7 0.0 slice-start
  2.7 0.2 broadcast_in_dim.24
  2.9 0.3 pad_maximum_fusion
  3.2 23.0 %all_to_all.20 = bf16[128,2,640]{2,1,0:T(2,128)(2,1)S(1)} all-to-all(bf16[128,2,640]{2,1,0:T(2,128)(2,1)S(1)} %bitcast.21), channel_id=1, replica_groups=mesh['zlo'=2,'core'=2,'x'=4,'zhi'=2,'y'=4] {'zlo','core','x','zhi','y'}, dimensions={0} | all-to-all | bytes 655360 | tf_op jit(solution)/shard_map/all_to_all | solution.py:153
  26.3 0.2 slice.17
  26.5 0.1 reshape.80.table_ref
  26.6 0.1 copy.17
  26.7 0.0 slice-start.1
  26.7 1.0 pick_slices.1
  27.7 0.0 copy-start
  27.7 0.0 copy-start.1
  27.8 0.0 copy-start.2
  27.8 0.0 copy-start.3
  27.8 0.0 copy-start.4
  27.8 44.5 %all_to_all.21.slices_ref = bf16[64,48,512]{2,1,0:T(8,128)(2,1)S(1)} all-to-all(bf16[64,48,512]{2,1,0:T(8,128)(2,1)S(1)} %pick_slices.1), channel_id=1, replica_groups=mesh['zlo'=2,'core'=2,'x'=4,'zhi'=2,'y'=4] {'zlo','core','x','y'}, dimensions={0} | all-to-all | bytes 6291456 | tf_op jit(solution)/shard_map/all_to_all | solution.py:160
  72.3 0.0 slice-done
  72.3 0.0 slice-done.1
  72.3 0.0 copy-done
  72.4 0.0 copy-done.1
  72.4 0.0 copy-done.2
  72.4 0.0 copy-done.3
  72.4 0.0 copy-done.4
  72.4 4.1 %layer.1 = (bf16[512,256]{1,0:T(8,128)(2,1)}, f32[128,384]{1,0:T(8,128)S(1)}) custom-call(s32[4,12]{1,0:T(4,128)S(1)} %copy-done.2, s32[4]{0:T(128)S(1)} %copy-done.4, bf16[4,12,256,256]{3,2,1,0:T(8,128)(2,1)S(1)} %bitcast.17, bf16[64,48,512]{2,1,0:T(8,128)(2,1)S(1)} %all_to_all.21.slices_ref, bf16[128,256]{1,0:T(8,128)(2,1)S(1)} %copy-done.1, ...), custom_call_target="tpu_custom_call" | custom-call | tf_op jit(solution)/shard_map/layer/pallas_call | solution.py:107
  76.5 0.2 copy.18
  76.7 14.8 %all_to_all.22 = f32[128,1,384]{2,1,0:T(1,128)S(1)} all-to-all(f32[128,1,384]{2,1,0:T(1,128)S(1)} %copy.18), channel_id=1, replica_groups=mesh['zlo'=2,'core'=2,'x'=4,'zhi'=2,'y'=4] {'zlo','core','x','zhi','y'}, dimensions={0} | all-to-all | bytes 393216 | tf_op jit(solution)/shard_map/all_to_all | solution.py:127
  91.5 0.2 reduce_sum.9
  91.7 0.1 broadcast_in_dim.27
  91.8 14.6 %all_to_all.23 = f32[128,1,384]{2,1,0:T(1,128)S(1)} all-to-all(f32[128,1,384]{2,1,0:T(1,128)S(1)} %broadcast_in_dim.27), channel_id=1, replica_groups=mesh['zlo'=2,'core'=2,'x'=4,'zhi'=2,'y'=4] {'zlo','core','x','zhi','y'}, dimensions={0} | all-to-all | bytes 393216 | tf_op jit(solution)/shard_map/all_to_all | solution.py:128
  106.4 0.6 slice_bitcast_fusion
  107.0 0.7 slice.18
  (10 shorter events, 0.2 us)
Async XLA Ops:
  2.7 69.6 %slice-start = ((s8[6291456]{0:T(1024)(128)(4,1)}), s8[2097152]{0:T(1024)(128)(4,1)S(1)}, s32[]{:S(2)}) async-start(s8[6291456]{0:T(1024)(128)(4,1)} %bitcast.16), calls=%async_computation.4 | async-start | bytes 4194304
  26.7 45.7 %slice-start.1 = ((s8[6291456]{0:T(1024)(128)(4,1)}), s8[4194304]{0:T(1024)(128)(4,1)S(1)}, s32[]{:S(2)}) async-start(s8[6291456]{0:T(1024)(128)(4,1)} %bitcast.16), calls=%async_computation.5 | async-start | bytes 8388608
  27.7 44.6 %copy-start = (bf16[512,256]{1,0:T(8,128)(2,1)S(1)}, bf16[512,256]{1,0:T(8,128)(2,1)}, u32[]{:S(2)}) copy-start(bf16[512,256]{1,0:T(8,128)(2,1)} %cotangent_ref.1) | copy-start | bytes 786436
  27.7 44.6 %copy-start.1 = (bf16[128,256]{1,0:T(8,128)(2,1)S(1)}, bf16[128,256]{1,0:T(8,128)(2,1)}, u32[]{:S(2)}) copy-start(bf16[128,256]{1,0:T(8,128)(2,1)} %weight_ref.1) | copy-start | bytes 196612
  27.8 44.6 %copy-start.2 = (s32[4,12]{1,0:T(4,128)S(1)}, s32[4,12]{1,0:T(4,128)}, u32[]{:S(2)}) copy-start(s32[4,12]{1,0:T(4,128)} %row_ref.1) | copy-start | bytes 580
  27.8 44.6 %copy-start.3 = (f32[256]{0:T(256)S(1)}, f32[256]{0:T(256)}, u32[]{:S(2)}) copy-start(f32[256]{0:T(256)} %param.14) | copy-start | bytes 3076
  27.8 44.6 %copy-start.4 = (s32[4]{0:T(128)S(1)}, s32[4]{0:T(128)}, u32[]{:S(2)}) copy-start(s32[4]{0:T(128)} %count_ref.1) | copy-start | bytes 52

commit v6 on v5

--- a/solution.py
+++ b/solution.py
@@ -16,6 +16,7 @@
 SPAN = 8
 RUN = 6
 LANES = 128
+PANEL = 2 * math.prod(AXIS_SIZES) // 4
 
 
 def pick_kernel(need_ref, table_ref, out_ref):
@@ -129,15 +130,42 @@
     return shared.reshape(grad.shape)
 
 
+def stage_kernel(features_ref, cols_ref, features_out, cols_out):
+    features_out[...] = features_ref[...]
+    groups, slots = cols_ref.shape
+    team = lax.broadcasted_iota(jnp.int32, (groups, slots), 0)
+    need = (team * PANEL + cols_ref[...]).astype(jnp.bfloat16)
+    row = jnp.zeros((1, LANES), jnp.float32)
+    for group in range(groups):
+        at = lax.broadcasted_iota(jnp.int32, (slots, LANES), 1)
+        own = lax.broadcasted_iota(jnp.int32, (slots, LANES), 0) + group * slots
+        put = jnp.where(at == own, 1.0, 0.0).astype(jnp.bfloat16)
+        row += jnp.dot(need[group : group + 1], put, preferred_element_type=jnp.float32)
+    cols_out[...] = row.astype(jnp.bfloat16)
+
+
+def stage(features, cols):
+    vmem = pl.BlockSpec(memory_space=pltpu.VMEM)
+    return pl.pallas_call(
+        stage_kernel,
+        out_shape=(
+            pltpu.VMEM(features.shape, features.dtype),
+            pltpu.VMEM((1, LANES), jnp.bfloat16),
+        ),
+        in_specs=[vmem, vmem],
+        out_specs=(vmem, vmem),
+        name="stage",
+    )(features, cols)
+
+
 def local(features, tile_values, tile_row, tile_col, tile_count, weight, bias, cotangent):
     groups, slots, block, _ = tile_values.shape
     width = features.shape[1]
     turns = block // PEERS
     needed = groups * slots
 
-    team = lax.broadcasted_iota(jnp.int32, (groups, slots), 0)
-    need = team * (2 * lax.axis_size(AXES) // groups) + tile_col
-    need = jnp.pad(need.astype(jnp.bfloat16).reshape(needed), (0, width - needed))
+    features, need = stage(features, tile_col)
+    need = need.reshape(width)
 
     mine = features.reshape(-1, turns, PEERS, width).transpose(2, 0, 1, 3).reshape(PEERS, -1, turns * width)
     grid = [SIZE[axis] for axis in AXES]

time: 108 us -> 107 us (level)
  no operation moved by 1% of the time
where the time goes in v6:
time: 107 us
  blocking collectives  97 us (91%)
  Pallas kernels  6.14 us (6%)
  local copies, waits for them, and re-layouts  2.36 us (2%)
    all_to_all x1, blocking collectives, local(): slices = lax.all_to_all(pick_slices(wanted, table), DEAL, 0, 0)  44.5 us
    all_to_all x1, blocking collectives, local(): lax.all_to_all(sent.reshape((-1,) + sent.shape[len(grid):]), AXES, 0, 0)  23 us
    all_to_all x1, blocking collectives, sum_over_devices(): total = jnp.sum(lax.all_to_all(rows, group, 0, 0), axis=0)  14.8 us
    all_to_all x1, blocking collectives, sum_over_devices(): lax.all_to_all(jnp.broadcast_to(total[None], rows.shape), group, 0, 0)  14.6 us
    pallas_call x1, Pallas kernels, layer(): pl.pallas_call(layer_kernel, out_shape=(jax.ShapeDtypeStruct((nodes, out_...  4.05 us

profile of v6, /device:TPU:1, one launch (start us, length us, event | category | flops | bytes accessed | tf_op | source)
XLA Modules:
  0.0 106.9 jit_solution(4545450406999966515)
XLA Ops:
  0.6 1.0 stage.1
  1.7 0.1 copy.24
  1.8 0.1 broadcast_in_dim.22
  1.9 0.1 broadcast_multiply_fusion
  2.0 0.0 slice-start
  2.0 0.2 broadcast_in_dim.23
  2.2 0.3 pad_maximum_fusion
  2.5 23.0 %all_to_all.20 = bf16[128,2,640]{2,1,0:T(2,128)(2,1)S(1)} all-to-all(bf16[128,2,640]{2,1,0:T(2,128)(2,1)S(1)} %bitcast.24), channel_id=1, replica_groups=mesh['zlo'=2,'core'=2,'x'=4,'zhi'=2,'y'=4] {'zlo','core','x','zhi','y'}, dimensions={0} | all-to-all | bytes 655360 | tf_op jit(solution)/shard_map/all_to_all | solution.py:181
  25.5 0.2 slice.17
  25.7 0.1 reshape.78.table_ref
  25.9 0.1 copy.17
  26.0 0.0 slice-start.1
  26.0 1.0 pick_slices.1
  27.0 0.0 copy-start
  27.0 0.0 copy-start.1
  27.0 0.0 copy-start.2
  27.0 0.0 copy-start.3
  27.1 0.0 copy-start.4
  27.1 44.5 %all_to_all.21.slices_ref = bf16[64,48,512]{2,1,0:T(8,128)(2,1)S(1)} all-to-all(bf16[64,48,512]{2,1,0:T(8,128)(2,1)S(1)} %pick_slices.1), channel_id=1, replica_groups=mesh['zlo'=2,'core'=2,'x'=4,'zhi'=2,'y'=4] {'zlo','core','x','y'}, dimensions={0} | all-to-all | bytes 6291456 | tf_op jit(solution)/shard_map/all_to_all | solution.py:188
  71.6 0.0 slice-done
  71.6 0.0 slice-done.1
  71.6 0.0 copy-done
  71.6 0.0 copy-done.1
  71.6 0.0 copy-done.2
  71.6 0.0 copy-done.3
  71.7 0.0 copy-done.4
  71.7 4.0 %layer.1 = (bf16[512,256]{1,0:T(8,128)(2,1)}, f32[128,384]{1,0:T(8,128)S(1)}) custom-call(s32[4,12]{1,0:T(4,128)S(1)} %copy-done.2, s32[4]{0:T(128)S(1)} %copy-done.4, bf16[4,12,256,256]{3,2,1,0:T(8,128)(2,1)S(1)} %bitcast.18, bf16[64,48,512]{2,1,0:T(8,128)(2,1)S(1)} %all_to_all.21.slices_ref, bf16[128,256]{1,0:T(8,128)(2,1)S(1)} %copy-done.1, ...), custom_call_target="tpu_custom_call" | custom-call | tf_op jit(solution)/shard_map/layer/pallas_call | solution.py:108
  75.7 0.2 copy.18
  75.9 14.8 %all_to_all.22 = f32[128,1,384]{2,1,0:T(1,128)S(1)} all-to-all(f32[128,1,384]{2,1,0:T(1,128)S(1)} %copy.18), channel_id=1, replica_groups=mesh['zlo'=2,'core'=2,'x'=4,'zhi'=2,'y'=4] {'zlo','core','x','zhi','y'}, dimensions={0} | all-to-all | bytes 393216 | tf_op jit(solution)/shard_map/all_to_all | solution.py:128
  90.8 0.2 reduce_sum.9
  90.9 0.1 broadcast_in_dim.26
  91.1 14.6 %all_to_all.23 = f32[128,1,384]{2,1,0:T(1,128)S(1)} all-to-all(f32[128,1,384]{2,1,0:T(1,128)S(1)} %broadcast_in_dim.26), channel_id=1, replica_groups=mesh['zlo'=2,'core'=2,'x'=4,'zhi'=2,'y'=4] {'zlo','core','x','zhi','y'}, dimensions={0} | all-to-all | bytes 393216 | tf_op jit(solution)/shard_map/all_to_all | solution.py:129
  105.7 0.6 slice_bitcast_fusion
  106.2 0.7 slice.18
  (8 shorter events, 0.2 us)
Async XLA Ops:
  2.0 69.6 %slice-start = ((s8[6291456]{0:T(1024)(128)(4,1)}), s8[2097152]{0:T(1024)(128)(4,1)S(1)}, s32[]{:S(2)}) async-start(s8[6291456]{0:T(1024)(128)(4,1)} %bitcast.17), calls=%async_computation.4 | async-start | bytes 4194304
  26.0 45.7 %slice-start.1 = ((s8[6291456]{0:T(1024)(128)(4,1)}), s8[4194304]{0:T(1024)(128)(4,1)S(1)}, s32[]{:S(2)}) async-start(s8[6291456]{0:T(1024)(128)(4,1)} %bitcast.17), calls=%async_computation.5 | async-start | bytes 8388608
  27.0 44.6 %copy-start = (bf16[512,256]{1,0:T(8,128)(2,1)S(1)}, bf16[512,256]{1,0:T(8,128)(2,1)}, u32[]{:S(2)}) copy-start(bf16[512,256]{1,0:T(8,128)(2,1)} %cotangent_ref.1) | copy-start | bytes 786436
  27.0 44.6 %copy-start.1 = (bf16[128,256]{1,0:T(8,128)(2,1)S(1)}, bf16[128,256]{1,0:T(8,128)(2,1)}, u32[]{:S(2)}) copy-start(bf16[128,256]{1,0:T(8,128)(2,1)} %weight_ref.1) | copy-start | bytes 196612
  27.0 44.6 %copy-start.2 = (s32[4,12]{1,0:T(4,128)S(1)}, s32[4,12]{1,0:T(4,128)}, u32[]{:S(2)}) copy-start(s32[4,12]{1,0:T(4,128)} %row_ref.1) | copy-start | bytes 580
  27.0 44.6 %copy-start.3 = (f32[256]{0:T(256)S(1)}, f32[256]{0:T(256)}, u32[]{:S(2)}) copy-start(f32[256]{0:T(256)} %param.14) | copy-start | bytes 3076
  27.1 44.6 %copy-start.4 = (s32[4]{0:T(128)S(1)}, s32[4]{0:T(128)}, u32[]{:S(2)}) copy-start(s32[4]{0:T(128)} %count_ref.1) | copy-start | bytes 52

commit v7 on v6

--- a/solution.py
+++ b/solution.py
@@ -134,12 +134,12 @@
     features_out[...] = features_ref[...]
     groups, slots = cols_ref.shape
     team = lax.broadcasted_iota(jnp.int32, (groups, slots), 0)
-    need = (team * PANEL + cols_ref[...]).astype(jnp.bfloat16)
+    need = (team * PANEL + cols_ref[...]).astype(jnp.float32)
     row = jnp.zeros((1, LANES), jnp.float32)
     for group in range(groups):
         at = lax.broadcasted_iota(jnp.int32, (slots, LANES), 1)
         own = lax.broadcasted_iota(jnp.int32, (slots, LANES), 0) + group * slots
-        put = jnp.where(at == own, 1.0, 0.0).astype(jnp.bfloat16)
+        put = jnp.where(at == own, 1.0, 0.0)
         row += jnp.dot(need[group : group + 1], put, preferred_element_type=jnp.float32)
     cols_out[...] = row.astype(jnp.bfloat16)
 

time: 107 us -> 107 us (level)
  no operation moved by 1% of the time
where the time goes in v7:
time: 107 us
  blocking collectives  97 us (91%)
  Pallas kernels  6.14 us (6%)
  local copies, waits for them, and re-layouts  2.36 us (2%)
    all_to_all x1, blocking collectives, local(): slices = lax.all_to_all(pick_slices(wanted, table), DEAL, 0, 0)  44.5 us
    all_to_all x1, blocking collectives, local(): lax.all_to_all(sent.reshape((-1,) + sent.shape[len(grid):]), AXES, 0, 0)  23 us
    all_to_all x1, blocking collectives, sum_over_devices(): total = jnp.sum(lax.all_to_all(rows, group, 0, 0), axis=0)  14.8 us
    all_to_all x1, blocking collectives, sum_over_devices(): lax.all_to_all(jnp.broadcast_to(total[None], rows.shape), group, 0, 0)  14.6 us
    pallas_call x1, Pallas kernels, layer(): pl.pallas_call(layer_kernel, out_shape=(jax.ShapeDtypeStruct((nodes, out_...  4.05 us

profile of v7, /device:TPU:1, one launch (start us, length us, event | category | flops | bytes accessed | tf_op | source)
XLA Modules:
  0.0 106.9 jit_solution(5867056192386812217)
XLA Ops:
  0.6 1.0 stage.1
  1.7 0.1 copy.24
  1.8 0.1 broadcast_in_dim.22
  1.9 0.1 broadcast_multiply_fusion
  2.0 0.0 slice-start
  2.0 0.2 broadcast_in_dim.23
  2.1 0.3 pad_maximum_fusion
  2.5 23.0 %all_to_all.20 = bf16[128,2,640]{2,1,0:T(2,128)(2,1)S(1)} all-to-all(bf16[128,2,640]{2,1,0:T(2,128)(2,1)S(1)} %bitcast.24), channel_id=1, replica_groups=mesh['zlo'=2,'core'=2,'x'=4,'zhi'=2,'y'=4] {'zlo','core','x','zhi','y'}, dimensions={0} | all-to-all | bytes 655360 | tf_op jit(solution)/shard_map/all_to_all | solution.py:181
  25.5 0.2 slice.17
  25.7 0.1 reshape.78.table_ref
  25.9 0.1 copy.17
  26.0 0.0 slice-start.1
  26.0 1.0 pick_slices.1
  27.0 0.0 copy-start
  27.0 0.0 copy-start.1
  27.0 0.0 copy-start.2
  27.0 0.0 copy-start.3
  27.1 0.0 copy-start.4
  27.1 44.5 %all_to_all.21.slices_ref = bf16[64,48,512]{2,1,0:T(8,128)(2,1)S(1)} all-to-all(bf16[64,48,512]{2,1,0:T(8,128)(2,1)S(1)} %pick_slices.1), channel_id=1, replica_groups=mesh['zlo'=2,'core'=2,'x'=4,'zhi'=2,'y'=4] {'zlo','core','x','y'}, dimensions={0} | all-to-all | bytes 6291456 | tf_op jit(solution)/shard_map/all_to_all | solution.py:188
  71.6 0.0 slice-done
  71.6 0.0 slice-done.1
  71.6 0.0 copy-done
  71.6 0.0 copy-done.1
  71.6 0.0 copy-done.2
  71.6 0.0 copy-done.3
  71.6 0.0 copy-done.4
  71.7 4.1 %layer.1 = (bf16[512,256]{1,0:T(8,128)(2,1)}, f32[128,384]{1,0:T(8,128)S(1)}) custom-call(s32[4,12]{1,0:T(4,128)S(1)} %copy-done.2, s32[4]{0:T(128)S(1)} %copy-done.4, bf16[4,12,256,256]{3,2,1,0:T(8,128)(2,1)S(1)} %bitcast.18, bf16[64,48,512]{2,1,0:T(8,128)(2,1)S(1)} %all_to_all.21.slices_ref, bf16[128,256]{1,0:T(8,128)(2,1)S(1)} %copy-done.1, ...), custom_call_target="tpu_custom_call" | custom-call | tf_op jit(solution)/shard_map/layer/pallas_call | solution.py:108
  75.7 0.2 copy.18
  75.9 14.8 %all_to_all.22 = f32[128,1,384]{2,1,0:T(1,128)S(1)} all-to-all(f32[128,1,384]{2,1,0:T(1,128)S(1)} %copy.18), channel_id=1, replica_groups=mesh['zlo'=2,'core'=2,'x'=4,'zhi'=2,'y'=4] {'zlo','core','x','zhi','y'}, dimensions={0} | all-to-all | bytes 393216 | tf_op jit(solution)/shard_map/all_to_all | solution.py:128
  90.8 0.2 reduce_sum.9
  90.9 0.1 broadcast_in_dim.26
  91.1 14.6 %all_to_all.23 = f32[128,1,384]{2,1,0:T(1,128)S(1)} all-to-all(f32[128,1,384]{2,1,0:T(1,128)S(1)} %broadcast_in_dim.26), channel_id=1, replica_groups=mesh['zlo'=2,'core'=2,'x'=4,'zhi'=2,'y'=4] {'zlo','core','x','zhi','y'}, dimensions={0} | all-to-all | bytes 393216 | tf_op jit(solution)/shard_map/all_to_all | solution.py:129
  105.7 0.6 slice_bitcast_fusion
  106.2 0.7 slice.18
  (8 shorter events, 0.2 us)
Async XLA Ops:
  2.0 69.6 %slice-start = ((s8[6291456]{0:T(1024)(128)(4,1)}), s8[2097152]{0:T(1024)(128)(4,1)S(1)}, s32[]{:S(2)}) async-start(s8[6291456]{0:T(1024)(128)(4,1)} %bitcast.17), calls=%async_computation.4 | async-start | bytes 4194304
  26.0 45.7 %slice-start.1 = ((s8[6291456]{0:T(1024)(128)(4,1)}), s8[4194304]{0:T(1024)(128)(4,1)S(1)}, s32[]{:S(2)}) async-start(s8[6291456]{0:T(1024)(128)(4,1)} %bitcast.17), calls=%async_computation.5 | async-start | bytes 8388608
  27.0 44.6 %copy-start = (bf16[512,256]{1,0:T(8,128)(2,1)S(1)}, bf16[512,256]{1,0:T(8,128)(2,1)}, u32[]{:S(2)}) copy-start(bf16[512,256]{1,0:T(8,128)(2,1)} %cotangent_ref.1) | copy-start | bytes 786436
  27.0 44.6 %copy-start.1 = (bf16[128,256]{1,0:T(8,128)(2,1)S(1)}, bf16[128,256]{1,0:T(8,128)(2,1)}, u32[]{:S(2)}) copy-start(bf16[128,256]{1,0:T(8,128)(2,1)} %weight_ref.1) | copy-start | bytes 196612
  27.0 44.6 %copy-start.2 = (s32[4,12]{1,0:T(4,128)S(1)}, s32[4,12]{1,0:T(4,128)}, u32[]{:S(2)}) copy-start(s32[4,12]{1,0:T(4,128)} %row_ref.1) | copy-start | bytes 580
  27.0 44.6 %copy-start.3 = (f32[256]{0:T(256)S(1)}, f32[256]{0:T(256)}, u32[]{:S(2)}) copy-start(f32[256]{0:T(256)} %param.14) | copy-start | bytes 3076
  27.1 44.6 %copy-start.4 = (s32[4]{0:T(128)S(1)}, s32[4]{0:T(128)}, u32[]{:S(2)}) copy-start(s32[4]{0:T(128)} %count_ref.1) | copy-start | bytes 52

commit v8 on v7

--- a/solution.py
+++ b/solution.py
@@ -130,7 +130,7 @@
     return shared.reshape(grad.shape)
 
 
-def stage_kernel(features_ref, cols_ref, features_out, cols_out):
+def stage_kernel(at_ref, features_ref, cols_ref, features_out, cols_out):
     features_out[...] = features_ref[...]
     groups, slots = cols_ref.shape
     team = lax.broadcasted_iota(jnp.int32, (groups, slots), 0)
@@ -141,21 +141,22 @@
         own = lax.broadcasted_iota(jnp.int32, (slots, LANES), 0) + group * slots
         put = jnp.where(at == own, 1.0, 0.0)
         row += jnp.dot(need[group : group + 1], put, preferred_element_type=jnp.float32)
-    cols_out[...] = row.astype(jnp.bfloat16)
+    place = lax.broadcasted_iota(jnp.int32, cols_out.shape, 0)
+    cols_out[...] = jnp.where(place == at_ref[0], row, 0.0).astype(jnp.bfloat16)
 
 
-def stage(features, cols):
+def stage(at, features, cols):
     vmem = pl.BlockSpec(memory_space=pltpu.VMEM)
     return pl.pallas_call(
         stage_kernel,
         out_shape=(
             pltpu.VMEM(features.shape, features.dtype),
-            pltpu.VMEM((1, LANES), jnp.bfloat16),
+            pltpu.VMEM((SIZE[ALIKE[0]], LANES), jnp.bfloat16),
         ),
-        in_specs=[vmem, vmem],
+        in_specs=[pl.BlockSpec(memory_space=pltpu.SMEM), vmem, vmem],
         out_specs=(vmem, vmem),
         name="stage",
-    )(features, cols)
+    )(at, features, cols)
 
 
 def local(features, tile_values, tile_row, tile_col, tile_count, weight, bias, cotangent):
@@ -164,19 +165,14 @@
     turns = block // PEERS
     needed = groups * slots
 
-    features, need = stage(features, tile_col)
-    need = need.reshape(width)
+    features, need = stage(lax.axis_index(ALIKE[0]).reshape(1), features, tile_col)
 
     mine = features.reshape(-1, turns, PEERS, width).transpose(2, 0, 1, 3).reshape(PEERS, -1, turns * width)
     grid = [SIZE[axis] for axis in AXES]
     once = [1 if axis in ALIKE else SIZE[axis] for axis in AXES]
     copies = [SIZE[axis] if axis in ALIKE else 1 for axis in AXES]
-    near = jnp.ones(copies + [1, 1], need.dtype)
-    for axis in ALIKE:
-        at = lax.broadcasted_iota(jnp.int32, near.shape, AXES.index(axis))
-        near = jnp.where(at == lax.axis_index(axis), near, 0)
     rows = jnp.broadcast_to(mine.reshape(once + list(mine.shape[1:])), grid + list(mine.shape[1:]))
-    lists = jnp.broadcast_to(need * near, grid + [mine.shape[1], width])
+    lists = jnp.broadcast_to(need.reshape(copies + [1, width]), grid + [mine.shape[1], width])
     sent = jnp.concatenate([rows, lists], axis=len(grid) + 1)
     dealt = lax.all_to_all(sent.reshape((-1,) + sent.shape[len(grid) :]), AXES, 0, 0)
     table = dealt[:, :, : turns * width].reshape(-1, turns * width)

time: 107 us -> 107 us (level)
  no operation moved by 1% of the time
where the time goes in v8:
time: 107 us
  blocking collectives  97 us (91%)
  Pallas kernels  6.13 us (6%)
  local copies, waits for them, and re-layouts  2.36 us (2%)
    all_to_all x1, blocking collectives, local(): slices = lax.all_to_all(pick_slices(wanted, table), DEAL, 0, 0)  44.5 us
    all_to_all x1, blocking collectives, local(): lax.all_to_all(sent.reshape((-1,) + sent.shape[len(grid):]), AXES, 0, 0)  23 us
    all_to_all x1, blocking collectives, sum_over_devices(): total = jnp.sum(lax.all_to_all(rows, group, 0, 0), axis=0)  14.8 us
    all_to_all x1, blocking collectives, sum_over_devices(): lax.all_to_all(jnp.broadcast_to(total[None], rows.shape), group, 0, 0)  14.6 us
    pallas_call x1, Pallas kernels, layer(): pl.pallas_call(layer_kernel, out_shape=(jax.ShapeDtypeStruct((nodes, out_...  4.05 us

profile of v8, /device:TPU:1, one launch (start us, length us, event | category | flops | bytes accessed | tf_op | source)
XLA Modules:
  0.0 106.8 jit_solution(3102514067581874190)
XLA Ops:
  0.6 1.0 stage.1
  1.7 0.1 copy.24
  1.8 0.1 broadcast_in_dim.8
  1.9 0.0 slice-start
  1.9 0.2 broadcast_in_dim.9
  2.1 0.3 pad_maximum_fusion
  2.4 23.0 %all_to_all.20 = bf16[128,2,640]{2,1,0:T(2,128)(2,1)S(1)} all-to-all(bf16[128,2,640]{2,1,0:T(2,128)(2,1)S(1)} %bitcast.23), channel_id=1, replica_groups=mesh['zlo'=2,'core'=2,'x'=4,'zhi'=2,'y'=4] {'zlo','core','x','zhi','y'}, dimensions={0} | all-to-all | bytes 655360 | tf_op jit(solution)/shard_map/all_to_all | solution.py:177
  25.4 0.2 slice.17
  25.6 0.1 reshape.43.table_ref
  25.8 0.1 copy.17
  25.9 0.0 slice-start.1
  25.9 1.0 pick_slices.1
  26.9 0.0 copy-start
  26.9 0.0 copy-start.1
  26.9 0.0 copy-start.2
  27.0 0.0 copy-start.3
  27.0 0.0 copy-start.4
  27.0 44.5 %all_to_all.21.slices_ref = bf16[64,48,512]{2,1,0:T(8,128)(2,1)S(1)} all-to-all(bf16[64,48,512]{2,1,0:T(8,128)(2,1)S(1)} %pick_slices.1), channel_id=1, replica_groups=mesh['zlo'=2,'core'=2,'x'=4,'zhi'=2,'y'=4] {'zlo','core','x','y'}, dimensions={0} | all-to-all | bytes 6291456 | tf_op jit(solution)/shard_map/all_to_all | solution.py:184
  71.5 0.0 slice-done
  71.5 0.0 slice-done.1
  71.5 0.0 copy-done
  71.5 0.0 copy-done.1
  71.5 0.0 copy-done.2
  71.6 0.0 copy-done.3
  71.6 0.0 copy-done.4
  71.6 4.1 %layer.1 = (bf16[512,256]{1,0:T(8,128)(2,1)}, f32[128,384]{1,0:T(8,128)S(1)}) custom-call(s32[4,12]{1,0:T(4,128)S(1)} %copy-done.2, s32[4]{0:T(128)S(1)} %copy-done.4, bf16[4,12,256,256]{3,2,1,0:T(8,128)(2,1)S(1)} %bitcast.18, bf16[64,48,512]{2,1,0:T(8,128)(2,1)S(1)} %all_to_all.21.slices_ref, bf16[128,256]{1,0:T(8,128)(2,1)S(1)} %copy-done.1, ...), custom_call_target="tpu_custom_call" | custom-call | tf_op jit(solution)/shard_map/layer/pallas_call | solution.py:108
  75.6 0.2 copy.18
  75.8 14.8 %all_to_all.22 = f32[128,1,384]{2,1,0:T(1,128)S(1)} all-to-all(f32[128,1,384]{2,1,0:T(1,128)S(1)} %copy.18), channel_id=1, replica_groups=mesh['zlo'=2,'core'=2,'x'=4,'zhi'=2,'y'=4] {'zlo','core','x','zhi','y'}, dimensions={0} | all-to-all | bytes 393216 | tf_op jit(solution)/shard_map/all_to_all | solution.py:128
  90.7 0.2 reduce_sum.9
  90.9 0.1 broadcast_in_dim.21
  91.0 14.6 %all_to_all.23 = f32[128,1,384]{2,1,0:T(1,128)S(1)} all-to-all(f32[128,1,384]{2,1,0:T(1,128)S(1)} %broadcast_in_dim.21), channel_id=1, replica_groups=mesh['zlo'=2,'core'=2,'x'=4,'zhi'=2,'y'=4] {'zlo','core','x','zhi','y'}, dimensions={0} | all-to-all | bytes 393216 | tf_op jit(solution)/shard_map/all_to_all | solution.py:129
  105.6 0.6 slice_bitcast_fusion
  106.1 0.7 slice.18
  (7 shorter events, 0.1 us)
Async XLA Ops:
  1.9 69.6 %slice-start = ((s8[6291456]{0:T(1024)(128)(4,1)}), s8[2097152]{0:T(1024)(128)(4,1)S(1)}, s32[]{:S(2)}) async-start(s8[6291456]{0:T(1024)(128)(4,1)} %bitcast.17), calls=%async_computation.4 | async-start | bytes 4194304
  25.9 45.7 %slice-start.1 = ((s8[6291456]{0:T(1024)(128)(4,1)}), s8[4194304]{0:T(1024)(128)(4,1)S(1)}, s32[]{:S(2)}) async-start(s8[6291456]{0:T(1024)(128)(4,1)} %bitcast.17), calls=%async_computation.5 | async-start | bytes 8388608
  26.9 44.6 %copy-start = (bf16[512,256]{1,0:T(8,128)(2,1)S(1)}, bf16[512,256]{1,0:T(8,128)(2,1)}, u32[]{:S(2)}) copy-start(bf16[512,256]{1,0:T(8,128)(2,1)} %cotangent_ref.1) | copy-start | bytes 786436
  26.9 44.6 %copy-start.1 = (bf16[128,256]{1,0:T(8,128)(2,1)S(1)}, bf16[128,256]{1,0:T(8,128)(2,1)}, u32[]{:S(2)}) copy-start(bf16[128,256]{1,0:T(8,128)(2,1)} %weight_ref.1) | copy-start | bytes 196612
  26.9 44.6 %copy-start.2 = (s32[4,12]{1,0:T(4,128)S(1)}, s32[4,12]{1,0:T(4,128)}, u32[]{:S(2)}) copy-start(s32[4,12]{1,0:T(4,128)} %row_ref.1) | copy-start | bytes 580
  27.0 44.6 %copy-start.3 = (f32[256]{0:T(256)S(1)}, f32[256]{0:T(256)}, u32[]{:S(2)}) copy-start(f32[256]{0:T(256)} %param.14) | copy-start | bytes 3076
  27.0 44.6 %copy-start.4 = (s32[4]{0:T(128)S(1)}, s32[4]{0:T(128)}, u32[]{:S(2)}) copy-start(s32[4]{0:T(128)} %count_ref.1) | copy-start | bytes 52

commit v9 on v8

--- a/solution.py
+++ b/solution.py
@@ -13,8 +13,8 @@
 ALIKE = ("zhi",)
 DEAL = tuple(axis for axis in AXES if axis not in ALIKE)
 PEERS = math.prod(SIZE[axis] for axis in DEAL)
-SPAN = 8
-RUN = 6
+SPAN = 32
+RUN = 12
 LANES = 128
 PANEL = 2 * math.prod(AXIS_SIZES) // 4
 

time: 107 us -> 107 us (level)
  no operation moved by 1% of the time
where the time goes in v9:
time: 107 us
  blocking collectives  97 us (91%)
  Pallas kernels  6.09 us (6%)
  local copies, waits for them, and re-layouts  2.36 us (2%)
    all_to_all x1, blocking collectives, local(): slices = lax.all_to_all(pick_slices(wanted, table), DEAL, 0, 0)  44.5 us
    all_to_all x1, blocking collectives, local(): lax.all_to_all(sent.reshape((-1,) + sent.shape[len(grid):]), AXES, 0, 0)  23 us
    all_to_all x1, blocking collectives, sum_over_devices(): total = jnp.sum(lax.all_to_all(rows, group, 0, 0), axis=0)  14.8 us
    all_to_all x1, blocking collectives, sum_over_devices(): lax.all_to_all(jnp.broadcast_to(total[None], rows.shape), group, 0, 0)  14.6 us
    pallas_call x1, Pallas kernels, layer(): pl.pallas_call(layer_kernel, out_shape=(jax.ShapeDtypeStruct((nodes, out_...  4.01 us

profile of v9, /device:TPU:1, one launch (start us, length us, event | category | flops | bytes accessed | tf_op | source)
XLA Modules:
  0.0 106.8 jit_solution(16473650391795065306)
XLA Ops:
  0.6 1.0 stage.1
  1.7 0.1 copy.24
  1.8 0.1 broadcast_in_dim.8
  1.9 0.0 slice-start
  1.9 0.2 broadcast_in_dim.9
  2.1 0.3 pad_maximum_fusion
  2.4 23.0 %all_to_all.20 = bf16[128,2,640]{2,1,0:T(2,128)(2,1)S(1)} all-to-all(bf16[128,2,640]{2,1,0:T(2,128)(2,1)S(1)} %bitcast.23), channel_id=1, replica_groups=mesh['zlo'=2,'core'=2,'x'=4,'zhi'=2,'y'=4] {'zlo','core','x','zhi','y'}, dimensions={0} | all-to-all | bytes 655360 | tf_op jit(solution)/shard_map/all_to_all | solution.py:177
  25.4 0.2 slice.17
  25.6 0.1 reshape.43.table_ref
  25.8 0.1 copy.17
  25.9 0.0 slice-start.1
  25.9 1.0 pick_slices.1
  26.9 0.0 copy-start
  26.9 0.0 copy-start.1
  26.9 0.0 copy-start.2
  26.9 0.0 copy-start.3
  27.0 0.0 copy-start.4
  27.0 44.5 %all_to_all.21.slices_ref = bf16[64,48,512]{2,1,0:T(8,128)(2,1)S(1)} all-to-all(bf16[64,48,512]{2,1,0:T(8,128)(2,1)S(1)} %pick_slices.1), channel_id=1, replica_groups=mesh['zlo'=2,'core'=2,'x'=4,'zhi'=2,'y'=4] {'zlo','core','x','y'}, dimensions={0} | all-to-all | bytes 6291456 | tf_op jit(solution)/shard_map/all_to_all | solution.py:184
  71.5 0.0 slice-done
  71.5 0.0 slice-done.1
  71.5 0.0 copy-done
  71.5 0.0 copy-done.1
  71.5 0.0 copy-done.2
  71.6 0.0 copy-done.3
  71.6 0.0 copy-done.4
  71.6 4.0 %layer.1 = (bf16[512,256]{1,0:T(8,128)(2,1)}, f32[128,384]{1,0:T(8,128)S(1)}) custom-call(s32[4,12]{1,0:T(4,128)S(1)} %copy-done.2, s32[4]{0:T(128)S(1)} %copy-done.4, bf16[4,12,256,256]{3,2,1,0:T(8,128)(2,1)S(1)} %bitcast.18, bf16[64,48,512]{2,1,0:T(8,128)(2,1)S(1)} %all_to_all.21.slices_ref, bf16[128,256]{1,0:T(8,128)(2,1)S(1)} %copy-done.1, ...), custom_call_target="tpu_custom_call" | custom-call | tf_op jit(solution)/shard_map/layer/pallas_call | solution.py:108
  75.6 0.2 copy.18
  75.8 14.8 %all_to_all.22 = f32[128,1,384]{2,1,0:T(1,128)S(1)} all-to-all(f32[128,1,384]{2,1,0:T(1,128)S(1)} %copy.18), channel_id=1, replica_groups=mesh['zlo'=2,'core'=2,'x'=4,'zhi'=2,'y'=4] {'zlo','core','x','zhi','y'}, dimensions={0} | all-to-all | bytes 393216 | tf_op jit(solution)/shard_map/all_to_all | solution.py:128
  90.6 0.2 reduce_sum.9
  90.8 0.1 broadcast_in_dim.21
  90.9 14.6 %all_to_all.23 = f32[128,1,384]{2,1,0:T(1,128)S(1)} all-to-all(f32[128,1,384]{2,1,0:T(1,128)S(1)} %broadcast_in_dim.21), channel_id=1, replica_groups=mesh['zlo'=2,'core'=2,'x'=4,'zhi'=2,'y'=4] {'zlo','core','x','zhi','y'}, dimensions={0} | all-to-all | bytes 393216 | tf_op jit(solution)/shard_map/all_to_all | solution.py:129
  105.5 0.6 slice_bitcast_fusion
  106.1 0.7 slice.18
  (7 shorter events, 0.1 us)
Async XLA Ops:
  1.9 69.6 %slice-start = ((s8[6291456]{0:T(1024)(128)(4,1)}), s8[2097152]{0:T(1024)(128)(4,1)S(1)}, s32[]{:S(2)}) async-start(s8[6291456]{0:T(1024)(128)(4,1)} %bitcast.17), calls=%async_computation.4 | async-start | bytes 4194304
  25.9 45.7 %slice-start.1 = ((s8[6291456]{0:T(1024)(128)(4,1)}), s8[4194304]{0:T(1024)(128)(4,1)S(1)}, s32[]{:S(2)}) async-start(s8[6291456]{0:T(1024)(128)(4,1)} %bitcast.17), calls=%async_computation.5 | async-start | bytes 8388608
  26.9 44.6 %copy-start = (bf16[512,256]{1,0:T(8,128)(2,1)S(1)}, bf16[512,256]{1,0:T(8,128)(2,1)}, u32[]{:S(2)}) copy-start(bf16[512,256]{1,0:T(8,128)(2,1)} %cotangent_ref.1) | copy-start | bytes 786436
  26.9 44.6 %copy-start.1 = (bf16[128,256]{1,0:T(8,128)(2,1)S(1)}, bf16[128,256]{1,0:T(8,128)(2,1)}, u32[]{:S(2)}) copy-start(bf16[128,256]{1,0:T(8,128)(2,1)} %weight_ref.1) | copy-start | bytes 196612
  26.9 44.6 %copy-start.2 = (s32[4,12]{1,0:T(4,128)S(1)}, s32[4,12]{1,0:T(4,128)}, u32[]{:S(2)}) copy-start(s32[4,12]{1,0:T(4,128)} %row_ref.1) | copy-start | bytes 580
  26.9 44.6 %copy-start.3 = (f32[256]{0:T(256)S(1)}, f32[256]{0:T(256)}, u32[]{:S(2)}) copy-start(f32[256]{0:T(256)} %param.14) | copy-start | bytes 3076
  27.0 44.6 %copy-start.4 = (s32[4]{0:T(128)S(1)}, s32[4]{0:T(128)}, u32[]{:S(2)}) copy-start(s32[4]{0:T(128)} %count_ref.1) | copy-start | bytes 52
